TPU v7x, 512 devices: a whole 4x8x8 slice. The times are simulated.
512 devices in a mesh: section: 8 (over x, core), expert: 64 (over z, y).
Axes of the slice: x: 4, y: 8, z: 8, core: 2. Of those that a mesh axis runs over, the one named last changes fastest.
Arguments:
- tokens: bfloat16 [8, 128, 3072], P('section'), may hold values from -6 to 6
- gains: bfloat16 [3072], replicated, may hold values from 0.25 to 1.75
- w_router: bfloat16 [3072, 8], replicated, may hold values from -0.109375 to 0.109375
- w_gate: bfloat16 [8, 3072, 8192], P('section', None, 'expert'), may hold values from -0.109375 to 0.109375
- w_up: bfloat16 [8, 3072, 8192], P('section', None, 'expert'), may hold values from -0.109375 to 0.109375
- w_down: bfloat16 [8, 3072, 8192], P('section', 'expert'), may hold values from -0.125 to 0.125
- routing: int32 [8, 128, 2], replicated, may hold values from 0 to 7, all different within a row; in each aligned block of 128 rows (0 to 127, 128 to 255, ..., all dimensions but the last counted through in order) at most 64 rows name the same one
Outputs:
- result: bfloat16 [8, 128, 3072], P('section', None, 'expert')
Inputs may be any that keep to these rules, and one draw needn't show every extreme that they name: `routing`: each token names two different experts. In each microbatch no expert is named by more than 64 tokens, a bound that some block reaches.
All inputs are finite; a program needn't handle non-finite values.
Results may differ from a plain program's by a relative error of at most 0.0056.
Values may be sent and summed in bfloat16 or wider, within the bound.
No kernel may reach another device: no remote copies, remote signals or barrier semaphores. Data moves between devices by JAX's collectives and lax.ppermute only.
A program may use at most 64 MiB of HBM per device.

v0:
```python
import jax
import jax.numpy as jnp
from jax import lax
from jax.sharding import PartitionSpec as P

CAP = 64


def passed_along(array, axis, by):
    size = lax.axis_size(axis)
    return lax.ppermute(array, axis, [(i, (i + by) % size) for i in range(size)])


def norm_rows(values, gain_row):
    widened = values.astype(jnp.float32)
    mean_sq = jnp.mean(widened * widened, axis=-1, keepdims=True)
    return (widened * lax.rsqrt(mean_sq + 1e-05) * gain_row.astype(jnp.float32)).astype(
        jnp.bfloat16
    )


def expert_shares(normed, router, expert_ids):
    logits = jnp.dot(normed, router, preferred_element_type=jnp.float32)
    labels = jnp.arange(logits.shape[1], dtype=jnp.int32)
    picked = jnp.sum(
        jnp.where(expert_ids[:, :, None] == labels[None, None, :], logits[:, None, :], 0.0), axis=2
    )
    margin = picked[:, 0] - picked[:, 1]
    return jnp.stack([jax.nn.sigmoid(margin), jax.nn.sigmoid(-margin)], axis=1)


def slot_tables(expert_ids, expert_id, shares):
    slot_ids = jnp.arange(CAP, dtype=jnp.int32)
    matched = expert_ids == expert_id
    chosen = jnp.any(matched, axis=1)
    ranking = jnp.cumsum(chosen.astype(jnp.int32)) - 1
    placing = jnp.logical_and(ranking[None, :] == slot_ids[:, None], chosen[None, :])
    weights = jnp.sum(jnp.where(matched, shares, 0.0), axis=1)
    spread = jnp.where(placing, weights[None, :], 0.0)
    return (placing, spread)


def pack_rows(placing, normed):
    return jnp.dot(placing.astype(jnp.bfloat16), normed, preferred_element_type=jnp.float32).astype(
        jnp.bfloat16
    )


def tile_hidden(packed, gate_tile, up_tile):
    gate_pre = jnp.dot(packed, gate_tile, preferred_element_type=jnp.float32)
    up_proj = jnp.dot(packed, up_tile, preferred_element_type=jnp.float32)
    return (jax.nn.silu(gate_pre) * up_proj).astype(jnp.bfloat16)


def make_adder(down_columns, piece):
    return lax.dot_general(
        piece, down_columns, (((1,), (1,)), ((), ())), preferred_element_type=jnp.float32
    )


def spread_back(spread, output):
    return jnp.dot(spread.T, output, precision=lax.Precision.HIGHEST)


def per_device(tokens, gains, w_router, w_gate, w_up, w_down, routing):
    sections = lax.axis_size("section")
    section_id = lax.axis_index("section")
    held_count = w_gate.shape[0]
    col_count = w_down.shape[1]
    current = tokens[0]
    row_count = current.shape[0]
    normed = norm_rows(current, gains)
    running = jnp.zeros((row_count, col_count), jnp.float32)
    moving = normed
    for turn_index in range(sections):
        micro_index = (section_id - turn_index) % sections
        expert_ids = lax.dynamic_index_in_dim(routing, micro_index, 0, keepdims=False)
        shares = expert_shares(moving, w_router, expert_ids)
        expert_id = section_id * held_count + 0
        placing, spread = slot_tables(expert_ids, expert_id, shares)
        hidden = tile_hidden(pack_rows(placing, moving), w_gate[0], w_up[0])
        output = make_adder(w_down[0], lax.all_gather(hidden, "expert", axis=1, tiled=True))
        running = running + spread_back(spread, output)
        running = passed_along(running, "section", 1)
        if turn_index + 1 < sections:
            moving = passed_along(moving, "section", 1)
    own_columns = lax.dynamic_slice_in_dim(
        current, lax.axis_index("expert") * col_count, col_count, 1
    )
    return (own_columns.astype(jnp.float32) + running).astype(jnp.bfloat16)[None]


def solution(mesh):
    in_specs = (
        P("section", None, None),
        P(),
        P(),
        P("section", None, "expert"),
        P("section", None, "expert"),
        P("section", "expert", None),
        P(),
    )
    out_specs = P("section", None, "expert")
    return jax.shard_map(
        per_device, mesh=mesh, in_specs=in_specs, out_specs=out_specs, check_vma=False
    )
```

profile of v0, /device:TPU:1, one launch (start us, length us, event | category | flops | bytes accessed | tf_op | source)
XLA Modules:
  0.0 657.4 jit_solution(9562395911212430775)
XLA Ops:
  12.3 2.6 collective-permute-start.1
  16.2 7.6 %collective-permute-done.1 = bf16[128,3072]{1,0:T(8,128)(2,1)} collective-permute-done((bf16[128,3072]{1,0:T(8,128)(2,1)S(1)}, bf16[128,3072]{1,0:T(8,128)(2,1)}, u32[]{:S(2)}, u32[]{:S(2)}) %collective-permute-start.1) | collective-permute-done | bytes 786464 | tf_op jit(solution)/shard_map/ppermute | solution.py:11
  27.1 2.6 collective-permute-start.3
  31.5 7.5 %collective-permute-done.3 = bf16[128,3072]{1,0:T(8,128)(2,1)S(1)} collective-permute-done((bf16[128,3072]{1,0:T(8,128)(2,1)}, bf16[128,3072]{1,0:T(8,128)(2,1)S(1)}, u32[]{:S(2)}, u32[]{:S(2)}) %collective-permute-start.3) | collective-permute-done | bytes 786464 | tf_op jit(solution)/shard_map/ppermute | solution.py:11
  42.0 2.4 collective-permute-start.5
  45.9 7.7 %collective-permute-done.5 = bf16[128,3072]{1,0:T(8,128)(2,1)S(1)} collective-permute-done((bf16[128,3072]{1,0:T(8,128)(2,1)}, bf16[128,3072]{1,0:T(8,128)(2,1)S(1)}, u32[]{:S(2)}, u32[]{:S(2)}) %collective-permute-start.5) | collective-permute-done | bytes 786464 | tf_op jit(solution)/shard_map/ppermute | solution.py:11
  57.0 2.4 collective-permute-start.7
  59.4 33.6 %all-gather.9.cloned.1.call-done = bf16[64,8192]{1,0:T(8,128)(2,1)} async-done(((bf16[64,128]{1,0:T(8,128)(2,1)}), bf16[64,8192]{1,0:T(8,128)(2,1)}) %all-gather.9.cloned.1.call-update) | async-done | bytes 1048592 | tf_op jit(solution)/shard_map/all_gather | solution.py:82
  93.0 1.7 fusion.25
  94.9 6.2 collective-permute-start
  104.2 67.2 %all-gather.11.cloned.1.call-done = bf16[64,8192]{1,0:T(8,128)(2,1)} async-done(((bf16[64,128]{1,0:T(8,128)(2,1)}), bf16[64,8192]{1,0:T(8,128)(2,1)}) %all-gather.11.cloned.1.call-update) | async-done | bytes 1048592 | tf_op jit(solution)/shard_map/all_gather | solution.py:82
  171.4 1.6 fusion.23
  173.3 6.3 collective-permute-start.2
  183.7 66.0 %all-gather.13.cloned.1.call-done = bf16[64,8192]{1,0:T(8,128)(2,1)} async-done(((bf16[64,128]{1,0:T(8,128)(2,1)}), bf16[64,8192]{1,0:T(8,128)(2,1)}) %all-gather.13.cloned.1.call-update) | async-done | bytes 1048592 | tf_op jit(solution)/shard_map/all_gather | solution.py:82
  249.7 1.6 fusion.21
  251.4 6.3 collective-permute-start.11
  259.4 7.5 %collective-permute-done.11 = bf16[128,3072]{1,0:T(8,128)(2,1)S(1)} collective-permute-done((bf16[128,3072]{1,0:T(8,128)(2,1)}, bf16[128,3072]{1,0:T(8,128)(2,1)S(1)}, u32[]{:S(2)}, u32[]{:S(2)}) %collective-permute-start.11) | collective-permute-done | bytes 786464 | tf_op jit(solution)/shard_map/ppermute | solution.py:11
  269.0 58.9 %all-gather.15.cloned.1.call-done = bf16[64,8192]{1,0:T(8,128)(2,1)} async-done(((bf16[64,128]{1,0:T(8,128)(2,1)}), bf16[64,8192]{1,0:T(8,128)(2,1)}) %all-gather.15.cloned.1.call-update) | async-done | bytes 1048592 | tf_op jit(solution)/shard_map/all_gather | solution.py:82
  327.9 1.7 fusion.19
  329.6 6.3 collective-permute-start.13
  336.5 8.3 %collective-permute-done.13 = bf16[128,3072]{1,0:T(8,128)(2,1)S(1)} collective-permute-done((bf16[128,3072]{1,0:T(8,128)(2,1)S(1)}, bf16[128,3072]{1,0:T(8,128)(2,1)S(1)}, u32[]{:S(2)}, u32[]{:S(2)}) %collective-permute-start.13) | collective-permute-done | bytes 786464 | tf_op jit(solution)/shard_map/ppermute | solution.py:11
  346.6 59.4 %all-gather.17.cloned.1.call-done = bf16[64,8192]{1,0:T(8,128)(2,1)} async-done(((bf16[64,128]{1,0:T(8,128)(2,1)}), bf16[64,8192]{1,0:T(8,128)(2,1)}) %all-gather.17.cloned.1.call-update) | async-done | bytes 1048592 | tf_op jit(solution)/shard_map/all_gather | solution.py:82
  406.1 1.6 fusion.17
  407.9 6.3 collective-permute-start.8
  414.6 69.7 %all-gather.19.cloned.1.call-done = bf16[64,8192]{1,0:T(8,128)(2,1)} async-done(((bf16[64,128]{1,0:T(8,128)(2,1)}), bf16[64,8192]{1,0:T(8,128)(2,1)}) %all-gather.19.cloned.1.call-update) | async-done | bytes 1048592 | tf_op jit(solution)/shard_map/all_gather | solution.py:82
  486.1 6.3 collective-permute-start.10
  492.3 70.2 %all-gather.21.cloned.1.call-done = bf16[64,8192]{1,0:T(8,128)(2,1)} async-done(((bf16[64,128]{1,0:T(8,128)(2,1)}), bf16[64,8192]{1,0:T(8,128)(2,1)}) %all-gather.21.cloned.1.call-update) | async-done | bytes 1048592 | tf_op jit(solution)/shard_map/all_gather | solution.py:82
  562.5 1.6 fusion.13
  564.4 6.3 collective-permute-start.12
  570.7 70.2 %all-gather.23.cloned.1.call-done = bf16[64,8192]{1,0:T(8,128)(2,1)} async-done(((bf16[64,128]{1,0:T(8,128)(2,1)}), bf16[64,8192]{1,0:T(8,128)(2,1)}) %all-gather.23.cloned.1.call-update) | async-done | bytes 1048592 | tf_op jit(solution)/shard_map/all_gather | solution.py:82
  640.9 1.6 fusion.11
  642.7 6.3 collective-permute-start.14
  (202 shorter events, 37.1 us)
Async XLA Ops:
  6.5 86.5 %all-gather.9.cloned.1.call-start = ((), (), s32[]{:S(2)}) async-start(), calls=%async_computation | async-start | bytes 1064960 | tf_op jit(solution)/shard_map/all_gather | solution.py:82
  12.2 159.2 %all-gather.11.cloned.1.call-start = ((), (), s32[]{:S(2)}) async-start(), calls=%async_computation.1 | async-start | bytes 1064960 | tf_op jit(solution)/shard_map/all_gather | solution.py:82
  12.3 11.5 %collective-permute-start.1 = (bf16[128,3072]{1,0:T(8,128)(2,1)S(1)}, bf16[128,3072]{1,0:T(8,128)(2,1)}, u32[]{:S(2)}, u32[]{:S(2)}) collective-permute-start(bf16[128,3072]{1,0:T(8,128)(2,1)S(1)} %fusion.2), channel_id=1, source_target_pairs={{0,64},{64,128},{128,192},{192,256},{256,320},{320,384},{384,448},... | collective-permute-start | bytes 2359304 | tf_op jit(solution)/shard_map/ppermute | solution.py:11
  26.4 223.3 %all-gather.13.cloned.1.call-start = ((), (), s32[]{:S(2)}) async-start(), calls=%async_computation.2 | async-start | bytes 1064960 | tf_op jit(solution)/shard_map/all_gather | solution.py:82
  27.1 11.8 %collective-permute-start.3 = (bf16[128,3072]{1,0:T(8,128)(2,1)}, bf16[128,3072]{1,0:T(8,128)(2,1)S(1)}, u32[]{:S(2)}, u32[]{:S(2)}) collective-permute-start(bf16[128,3072]{1,0:T(8,128)(2,1)} %collective-permute-done.1), channel_id=1, source_target_pairs={{0,64},{64,128},{128,192},{192,256},{256,320},{320,384},{384,448},... | collective-permute-start | bytes 2359304 | tf_op jit(solution)/shard_map/ppermute | solution.py:11
  41.1 286.8 %all-gather.15.cloned.1.call-start = ((), (), s32[]{:S(2)}) async-start(), calls=%async_computation.3 | async-start | bytes 1064960 | tf_op jit(solution)/shard_map/all_gather | solution.py:82
  42.0 11.6 %collective-permute-start.5 = (bf16[128,3072]{1,0:T(8,128)(2,1)}, bf16[128,3072]{1,0:T(8,128)(2,1)S(1)}, u32[]{:S(2)}, u32[]{:S(2)}) collective-permute-start(bf16[128,3072]{1,0:T(8,128)(2,1)} %copy-done.5), channel_id=1, source_target_pairs={{0,64},{64,128},{128,192},{192,256},{256,320},{320,384},{384,448},... | collective-permute-start | bytes 2359304 | tf_op jit(solution)/shard_map/ppermute | solution.py:11
  54.5 38.5 %copy-start.1 = (bf16[1,48,8192]{2,1,0:T(8,128)(2,1)S(1)}, bf16[1,48,8192]{2,1,0:T(8,128)(2,1)}, u32[]{:S(2)}) copy-start(bf16[1,48,8192]{2,1,0:T(8,128)(2,1)} %param.12) | copy-start | bytes 2359300
  55.4 350.6 %all-gather.17.cloned.1.call-start = ((), (), s32[]{:S(2)}) async-start(), calls=%async_computation.4 | async-start | bytes 1064960 | tf_op jit(solution)/shard_map/all_gather | solution.py:82
  57.0 44.5 %collective-permute-start.7 = (bf16[128,3072]{1,0:T(8,128)(2,1)}, bf16[128,3072]{1,0:T(8,128)(2,1)}, u32[]{:S(2)}, u32[]{:S(2)}) collective-permute-start(bf16[128,3072]{1,0:T(8,128)(2,1)} %copy-done.8), channel_id=1, source_target_pairs={{0,64},{64,128},{128,192},{192,256},{256,320},{320,384},{384,448},... | collective-permute-start | bytes 2359304 | tf_op jit(solution)/shard_map/ppermute | solution.py:11
  59.4 42.1 %copy-start.22 = (pred[128]{0:T(512)(128)(4,1)S(1)}, pred[128]{0:T(512)(128)(4,1)}, u32[]{:S(2)}) copy-start(pred[128]{0:T(512)(128)(4,1)} %copy-done.21) | copy-start | bytes 388
  94.9 78.1 %collective-permute-start = (f32[128,48]{0,1:T(8,128)S(1)}, f32[128,48]{0,1:T(8,128)S(1)}, u32[]{:S(2)}, u32[]{:S(2)}) collective-permute-start(f32[128,48]{0,1:T(8,128)S(1)} %fusion.64), channel_id=1, source_target_pairs={{0,64},{64,128},{128,192},{192,256},{256,320},{320,384},{384,448},... | collective-permute-start | bytes 73736 | tf_op jit(solution)/shard_map/ppermute | solution.py:11
  104.0 69.0 %copy-start.14 = (s32[128]{0:T(128)S(1)}, s32[128]{0:T(128)}, u32[]{:S(2)}) copy-start(s32[128]{0:T(128)} %copy-done.13) | copy-start | bytes 1540
  104.0 69.0 %copy-start.28 = (pred[128]{0:T(512)(128)(4,1)S(1)}, pred[128]{0:T(512)(128)(4,1)}, u32[]{:S(2)}) copy-start(pred[128]{0:T(512)(128)(4,1)} %copy-done.27) | copy-start | bytes 388
  104.1 380.2 %all-gather.19.cloned.1.call-start = ((), (), s32[]{:S(2)}) async-start(), calls=%async_computation.5 | async-start | bytes 1064960 | tf_op jit(solution)/shard_map/all_gather | solution.py:82
  104.2 76.8 %copy-start.20 = (pred[128]{0:T(512)(128)(4,1)S(1)}, pred[128]{0:T(512)(128)(4,1)}, u32[]{:S(2)}) copy-start(pred[128]{0:T(512)(128)(4,1)} %get-tuple-element.29) | copy-start | bytes 388
  104.2 76.8 %collective-permute-start.9 = (bf16[128,3072]{1,0:T(8,128)(2,1)}, bf16[128,3072]{1,0:T(8,128)(2,1)}, u32[]{:S(2)}, u32[]{:S(2)}) collective-permute-start(bf16[128,3072]{1,0:T(8,128)(2,1)} %collective-permute-done.7), channel_id=1, source_target_pairs={{0,64},{64,128},{128,192},{192,256},{256,320},{320,384},{384,448},... | collective-permute-start | bytes 2359304 | tf_op jit(solution)/shard_map/ppermute | solution.py:11
  173.3 84.6 %collective-permute-start.2 = (f32[128,48]{0,1:T(8,128)S(1)}, f32[128,48]{0,1:T(8,128)S(1)}, u32[]{:S(2)}, u32[]{:S(2)}) collective-permute-start(f32[128,48]{0,1:T(8,128)S(1)} %convolution_add_fusion), channel_id=1, source_target_pairs={{0,64},{64,128},{128,192},{192,256},{256,320},{320,384},{384,448},... | collective-permute-start | bytes 73736 | tf_op jit(solution)/shard_map/ppermute | solution.py:11
  183.6 74.1 %copy-start.26 = (pred[128]{0:T(512)(128)(4,1)S(1)}, pred[128]{0:T(512)(128)(4,1)}, u32[]{:S(2)}) copy-start(pred[128]{0:T(512)(128)(4,1)} %copy-done.25) | copy-start | bytes 388
  183.6 378.9 %all-gather.21.cloned.1.call-start = ((), (), s32[]{:S(2)}) async-start(), calls=%async_computation.6 | async-start | bytes 1064960 | tf_op jit(solution)/shard_map/all_gather | solution.py:82
  183.7 83.2 %copy-start.18 = (pred[128]{0:T(512)(128)(4,1)S(1)}, pred[128]{0:T(512)(128)(4,1)}, u32[]{:S(2)}) copy-start(pred[128]{0:T(512)(128)(4,1)} %get-tuple-element.31) | copy-start | bytes 388
  251.4 15.5 %collective-permute-start.11 = (bf16[128,3072]{1,0:T(8,128)(2,1)}, bf16[128,3072]{1,0:T(8,128)(2,1)S(1)}, u32[]{:S(2)}, u32[]{:S(2)}) collective-permute-start(bf16[128,3072]{1,0:T(8,128)(2,1)} %collective-permute-done.9), channel_id=1, source_target_pairs={{0,64},{64,128},{128,192},{192,256},{256,320},{320,384},{384,448},... | collective-permute-start | bytes 2359304 | tf_op jit(solution)/shard_map/ppermute | solution.py:11
  257.8 78.2 %collective-permute-start.4 = (f32[128,48]{0,1:T(8,128)S(1)}, f32[128,48]{0,1:T(8,128)S(1)}, u32[]{:S(2)}, u32[]{:S(2)}) collective-permute-start(f32[128,48]{0,1:T(8,128)S(1)} %add.251), channel_id=1, source_target_pairs={{0,64},{64,128},{128,192},{192,256},{256,320},{320,384},{384,448},... | collective-permute-start | bytes 73736 | tf_op jit(solution)/shard_map/ppermute | solution.py:11
  268.7 372.2 %all-gather.23.cloned.1.call-start = ((), (), s32[]{:S(2)}) async-start(), calls=%async_computation.7 | async-start | bytes 1064960 | tf_op jit(solution)/shard_map/all_gather | solution.py:82
  269.0 75.9 %copy-start.17 = (pred[128]{0:T(512)(128)(4,1)S(1)}, pred[128]{0:T(512)(128)(4,1)}, u32[]{:S(2)}) copy-start(pred[128]{0:T(512)(128)(4,1)} %get-tuple-element.5) | copy-start | bytes 388
  329.6 15.2 %collective-permute-start.13 = (bf16[128,3072]{1,0:T(8,128)(2,1)S(1)}, bf16[128,3072]{1,0:T(8,128)(2,1)S(1)}, u32[]{:S(2)}, u32[]{:S(2)}) collective-permute-start(bf16[128,3072]{1,0:T(8,128)(2,1)S(1)} %copy-done.7), channel_id=1, source_target_pairs={{0,64},{64,128},{128,192},{192,256},{256,320},{320,384},{384,448},... | collective-permute-start | bytes 2359304 | tf_op jit(solution)/shard_map/ppermute | solution.py:11
  336.1 71.8 %collective-permute-start.6 = (f32[128,48]{0,1:T(8,128)S(1)}, f32[128,48]{0,1:T(8,128)S(1)}, u32[]{:S(2)}, u32[]{:S(2)}) collective-permute-start(f32[128,48]{0,1:T(8,128)S(1)} %add.257), channel_id=1, source_target_pairs={{0,64},{64,128},{128,192},{192,256},{256,320},{320,384},{384,448},... | collective-permute-start | bytes 73736 | tf_op jit(solution)/shard_map/ppermute | solution.py:11
  346.6 67.6 %copy-start.11 = (bf16[128,3072]{1,0:T(8,128)(2,1)S(1)}, bf16[128,3072]{1,0:T(8,128)(2,1)}, u32[]{:S(2)}) copy-start(bf16[128,3072]{1,0:T(8,128)(2,1)} %copy-done.10) | copy-start | bytes 2359300
  407.9 78.1 %collective-permute-start.8 = (f32[128,48]{0,1:T(8,128)S(1)}, f32[128,48]{0,1:T(8,128)S(1)}, u32[]{:S(2)}, u32[]{:S(2)}) collective-permute-start(f32[128,48]{0,1:T(8,128)S(1)} %add.263), channel_id=1, source_target_pairs={{0,64},{64,128},{128,192},{192,256},{256,320},{320,384},{384,448},... | collective-permute-start | bytes 73736 | tf_op jit(solution)/shard_map/ppermute | solution.py:11
  486.1 78.3 %collective-permute-start.10 = (f32[128,48]{0,1:T(8,128)S(1)}, f32[128,48]{0,1:T(8,128)S(1)}, u32[]{:S(2)}, u32[]{:S(2)}) collective-permute-start(f32[128,48]{0,1:T(8,128)S(1)} %add.269), channel_id=1, source_target_pairs={{0,64},{64,128},{128,192},{192,256},{256,320},{320,384},{384,448},... | collective-permute-start | bytes 73736 | tf_op jit(solution)/shard_map/ppermute | solution.py:11
  564.4 78.3 %collective-permute-start.12 = (f32[128,48]{0,1:T(8,128)S(1)}, f32[128,48]{0,1:T(8,128)S(1)}, u32[]{:S(2)}, u32[]{:S(2)}) collective-permute-start(f32[128,48]{0,1:T(8,128)S(1)} %add.275), channel_id=1, source_target_pairs={{0,64},{64,128},{128,192},{192,256},{256,320},{320,384},{384,448},... | collective-permute-start | bytes 73736 | tf_op jit(solution)/shard_map/ppermute | solution.py:11
  642.7 7.2 %collective-permute-start.14 = (f32[128,48]{0,1:T(8,128)S(1)}, f32[128,48]{0,1:T(8,128)S(1)}, u32[]{:S(2)}, u32[]{:S(2)}) collective-permute-start(f32[128,48]{0,1:T(8,128)S(1)} %add.281), channel_id=1, source_target_pairs={{0,64},{64,128},{128,192},{192,256},{256,320},{320,384},{384,448},... | collective-permute-start | bytes 73736 | tf_op jit(solution)/shard_map/ppermute | solution.py:11
  (22 other events, 163.7 us)
Sparse Core Ops, SparseCore 0:
  12.3 80.6 all-gather.8
  96.0 75.3 all-gather.10
  174.4 75.2 all-gather.12
  252.6 75.2 all-gather.14
  330.7 75.2 all-gather.16
  408.9 75.2 all-gather.18
  487.2 75.2 all-gather.20
  565.5 75.2 all-gather.22
where the time goes:
time: 659 us; the launch traced here: 657 us
  waiting for transfers between devices  535 us (81%)
  starting transfers between devices  60.7 us (9%)
  matrix products  36.7 us (6%)
  between operations  14.5 us (2%)
  other arithmetic  7.7 us (1%)
    all_gather x8, waiting for transfers between devices, per_device(): lax.all_gather(hidden, 'expert', axis=1, tiled=True)  495 us
    ppermute x15, starting transfers between devices, passed_along(): lax.ppermute(array, axis, [(i, (i + by) % size) for i in range(size)])  60.2 us
    ppermute x15, waiting for transfers between devices, passed_along(): lax.ppermute(array, axis, [(i, (i + by) % size) for i in range(size)])  39.6 us
    dot_general x8, matrix products, make_adder(): lax.dot_general(piece, down_columns, (((1,), (1,)), ((), ())), preferred_...  13.2 us
  transfers between devices with their start and end apart: 23, of which 14 were waited for; matrix products, arithmetic and copies ran while one was open for 6% of the time, Pallas kernels for 0%

commit v1 on v0

v1 whole, which is shorter than its diff:
```python
import functools

import jax
import jax.numpy as jnp
from jax import lax
from jax.experimental import pallas as pl
from jax.experimental.pallas import tpu as pltpu
from jax.sharding import PartitionSpec as P

CAP = 64
CHIPS = 4
RING = 8
EXPERTS = 2 * CHIPS
HOPS = ((0, 0), (1, 0), (3, 0), (1, 1), (3, 1), (0, 1), (2, 0), (2, 1))
NEAR = 6
NEAR_FLOPS, FAR_FLOPS = 2**34, 2**28
AXES = ("section", "expert")
bf16, f32 = jnp.bfloat16, jnp.float32


def params(mib):
    return pltpu.CompilerParams(vmem_limit_bytes=mib * 2**20)


def call(kernel, out_shape, mib, flops=0, nbytes=0):
    return pl.pallas_call(
        kernel,
        out_shape=out_shape,
        compiler_params=params(mib),
        cost_estimate=pl.CostEstimate(flops=flops, bytes_accessed=nbytes, transcendentals=0),
    )


def towards(section, hop, sign):
    x, core = section // 2, section % 2
    return 2 * ((x + sign * hop[0]) % CHIPS) + (core + hop[1]) % 2


def hop_along(array, hop):
    return lax.ppermute(array, "section", [(i, towards(i, hop, 1)) for i in range(EXPERTS)])


def ring_groups():
    def place(section, z, y):
        return section * RING * RING + z * RING + y

    gather, reduce = [], []
    for section in range(EXPERTS):
        for u in range(RING):
            by_z = [place(section, v, u) for v in range(RING)]
            by_y = [place(section, u, v) for v in range(RING)]
            gather.append(by_y if section % 2 else by_z)
            reduce.append(by_z if section % 2 else by_y)
    return gather, reduce


def prep_kernel(tok_ref, gain_ref, router_ref, routing_ref, weight_ref, rank_ref, *packed_refs):
    section = lax.axis_index("section")
    rows = tok_ref.shape[0]
    x = tok_ref[...].astype(f32)
    mean_sq = jnp.mean(x * x, axis=-1, keepdims=True)
    normed = (x * lax.rsqrt(mean_sq + 1e-05) * gain_ref[...].astype(f32)).astype(bf16)

    ids = routing_ref[section]
    labels = lax.broadcasted_iota(jnp.int32, (EXPERTS, rows), 0)
    is_first, is_second = labels == ids[0:1], labels == ids[1:2]
    chosen = jnp.where(is_first | is_second, 1.0, 0.0)
    tall = lax.broadcasted_iota(jnp.int32, (rows, rows), 0)
    wide = lax.broadcasted_iota(jnp.int32, (rows, rows), 1)
    upto = jnp.where(tall <= wide, 1.0, 0.0).astype(bf16)
    ranks = jnp.dot(chosen.astype(bf16), upto, preferred_element_type=f32)
    rank_ref[...] = jnp.where(chosen > 0.0, ranks - 1.0, -1.0)
    slots = lax.broadcasted_iota(jnp.int32, (CAP, rows), 0).astype(f32)
    placing = jnp.concatenate(
        [
            jnp.where(slots == rank_ref[pl.ds(towards(section, hop, 1), 1), :], 1.0, 0.0)
            for hop in HOPS
        ],
        axis=0,
    ).astype(bf16)
    packed = jnp.dot(placing, normed, preferred_element_type=f32).astype(bf16)
    for k, ref in enumerate(packed_refs):
        ref[...] = packed[k * CAP : (k + 1) * CAP]

    logits = lax.dot_general(
        router_ref[...], normed, (((1,), (1,)), ((), ())), preferred_element_type=f32
    )
    margin = jnp.sum(jnp.where(is_first, logits, 0.0), axis=0, keepdims=True) - jnp.sum(
        jnp.where(is_second, logits, 0.0), axis=0, keepdims=True
    )
    weight_ref[...] = jnp.where(
        is_first, jax.nn.sigmoid(margin), jnp.where(is_second, jax.nn.sigmoid(-margin), 0.0)
    )


def regroup_kernel(down_ref, _, out_ref):
    swap = lax.axis_index("section") % 2
    major, minor = jnp.where(swap == 1, RING, 1), jnp.where(swap == 1, 1, RING)
    for p in range(RING):
        for q in range(RING):
            at = pl.multiple_of((p * major + q * minor) * 128, 128)
            out_ref[p, :, q * 128 : (q + 1) * 128] = down_ref[:, pl.ds(at, 128)]


def hidden_rows(gate_ref, up_ref, packed_refs):
    depth, width = gate_ref.shape
    step = 256
    total = None
    for at in range(0, depth, step):
        left = jnp.concatenate([ref[:, at : at + step] for ref in packed_refs], axis=0)
        right = jnp.concatenate([gate_ref[at : at + step], up_ref[at : at + step]], axis=1)
        term = jnp.dot(left, right, preferred_element_type=f32)
        total = term if total is None else total + term
    return (jax.nn.silu(total[:, :width]) * total[:, width:]).astype(bf16)


def near_kernel(gate_ref, up_ref, *rest):
    rest[-1][...] = hidden_rows(gate_ref, up_ref, rest[:-1])


def far_kernel(gate_ref, up_ref, near_ref, *rest):
    split, out_ref = near_ref.shape[0], rest[-1]
    near, far = near_ref[...], hidden_rows(gate_ref, up_ref, rest[:-1])
    for p in range(RING):
        out_ref[p, :split] = near
        out_ref[p, split:] = far


def project_kernel(down_ref, hidden_ref, out_ref):
    blocks, cols, depth = down_ref.shape
    width = hidden_ref.shape[2]
    total = None
    for q in range(0, RING, 2):
        left = down_ref[:, :, q * width : (q + 2) * width].reshape(blocks * cols, 2 * width)
        right = jnp.concatenate([hidden_ref[q], hidden_ref[q + 1]], axis=1)
        term = lax.dot_general(left, right, (((1,), (1,)), ((), ())), preferred_element_type=f32)
        total = term if total is None else total + term
    out_ref[...] = total.astype(bf16).reshape(blocks, cols, -1)


def sum_kernel(parts_ref, out_ref):
    section = lax.axis_index("section")
    total = jnp.sum(parts_ref[...].astype(f32), axis=0).astype(bf16)
    for k, hop in enumerate(HOPS):
        block = total[:, k * CAP : (k + 1) * CAP]
        out_ref[towards(section, hop, -1)] = jnp.concatenate([block, block], axis=1)


def combine_kernel(outputs_ref, weight_ref, rank_ref, own_ref, out_ref):
    rows = own_ref.shape[1]
    slots = lax.broadcasted_iota(jnp.int32, (CAP, rows), 0).astype(f32)
    total = own_ref[...].astype(f32)
    for e in range(EXPERTS):
        placing = jnp.where(slots == rank_ref[e : e + 1, :], 1.0, 0.0).astype(bf16)
        picked = jnp.dot(outputs_ref[e, :, :CAP], placing, preferred_element_type=f32)
        total = total + weight_ref[e : e + 1, :] * picked
    out_ref[...] = total.astype(bf16)


def per_device(tokens, gains, w_router, w_gate, w_up, w_down, routing):
    gather_groups, reduce_groups = ring_groups()
    exchange = functools.partial(
        lax.all_to_all, axis_name=AXES, split_axis=0, concat_axis=0
    )
    rows, depth = tokens.shape[1:]
    width, cols = w_gate.shape[2], w_down.shape[1]
    shape = jax.ShapeDtypeStruct
    block = shape((CAP, depth), bf16)

    weight, rank, *packed = pl.pallas_call(
        prep_kernel,
        out_shape=[shape((EXPERTS, rows), f32)] * 2 + [block] * len(HOPS),
        compiler_params=params(16),
    )(tokens[0], gains[None], w_router.T, jnp.swapaxes(routing, 1, 2))
    arrived = [packed[0]] + [
        hop_along(array, hop) for array, hop in zip(packed[1:], HOPS[1:], strict=True)
    ]

    down = call(regroup_kernel, shape((RING, cols, RING * width), bf16), 8)(w_down[0], rank)
    down = exchange(down, axis_index_groups=reduce_groups)

    slots = len(HOPS) * CAP
    hidden = call(near_kernel, shape((NEAR * CAP, width), bf16), 16, NEAR_FLOPS, 2**22)(
        w_gate[0], w_up[0], *arrived[:NEAR]
    )
    hidden = call(far_kernel, shape((RING, slots, width), bf16), 16, FAR_FLOPS, 2**22)(
        w_gate[0], w_up[0], hidden, *arrived[NEAR:]
    )
    hidden = exchange(hidden, axis_index_groups=gather_groups)
    parts = call(project_kernel, shape((RING, cols, slots), bf16), 16, 2**29, 2**21)(down, hidden)
    parts = exchange(parts, axis_index_groups=reduce_groups)
    outputs = call(sum_kernel, shape((EXPERTS, cols, 2 * CAP), bf16), 8)(parts)
    outputs = lax.all_to_all(outputs, "section", 0, 0)
    own = lax.dynamic_slice_in_dim(tokens[0], lax.axis_index("expert") * cols, cols, 1)
    result = call(combine_kernel, shape((cols, rows), bf16), 8)(outputs, weight, rank, own.T)
    return result.T[None]


def solution(mesh):
    in_specs = (
        P("section", None, None),
        P(),
        P(),
        P("section", None, "expert"),
        P("section", None, "expert"),
        P("section", "expert", None),
        P(),
    )
    out_specs = P("section", None, "expert")
    return jax.shard_map(
        per_device, mesh=mesh, in_specs=in_specs, out_specs=out_specs, check_vma=False
    )
```

time: 659 us -> 114 us (0.17)
  waiting for transfers between devices: 535 us -> 27.3 us
  matrix products: 36.7 us -> 0 us
  blocking collectives: 0 us -> 24.4 us
  between operations: 14.5 us -> 0.17 us
  starting transfers between devices: 60.7 us -> 46.6 us
  Pallas kernels: 0 us -> 9.27 us
  other arithmetic: 7.7 us -> 0 us
    all_gather x8 -> x0, waiting for transfers between devices: 495 us -> none  [per_device(): lax.all_gather(hidden, 'expert', axis=1, tiled=True)]
    dot_general x48 -> x0, matrix products: 36.7 us -> none  [the longest x8 13.2 us: make_adder(): lax.dot_general(piece, down_columns, (((1,), (1,)), ((), ())), preferred_...]
    ppermute x15 -> x7, starting transfers between devices: 60.2 us -> 28.5 us  [hop_along(): lax.ppermute(array, 'section', [(i, towards(i, hop, 1)) for i in range(EX...]
    ppermute x15 -> x7, waiting for transfers between devices: 39.6 us -> 12.6 us  [hop_along(): lax.ppermute(array, 'section', [(i, towards(i, hop, 1)) for i in range(EX...]
    all_to_all x0 -> x1, blocking collectives: none -> 24.4 us  [per_device(): hidden = exchange(hidden, axis_index_groups=gather_groups)]
    all_to_all x0 -> x3, starting transfers between devices: none -> 18.1 us  [the longest x1 7.53 us: per_device(): parts = exchange(parts, axis_index_groups=reduce_groups)]
    all_to_all x0 -> x3, waiting for transfers between devices: none -> 14.7 us  [the longest x1 10.7 us: per_device(): parts = exchange(parts, axis_index_groups=reduce_groups)]
    pallas_call x0 -> x7, Pallas kernels: none -> 9.27 us  [the longest x1 2.62 us: per_device(): pl.pallas_call(prep_kernel, out_shape=[shape((EXPERTS, rows), f32)] * 2 +...]
  transfers between devices with their start and end apart: 23 -> 10, of which waited for: 14 -> 4; matrix products, arithmetic and copies ran while one was open for 6% -> 1% of each run, Pallas kernels for 0% -> 3%
where the time goes in v1:
time: 114 us; the launch traced here: 113 us
  starting transfers between devices  46.6 us (41%)
  waiting for transfers between devices  27.3 us (24%)
  blocking collectives  24.4 us (21%)
  Pallas kernels  9.27 us (8%)
  local copies, waits for them, and re-layouts  5.39 us (5%)
    ppermute x7, starting transfers between devices, hop_along(): lax.ppermute(array, 'section', [(i, towards(i, hop, 1)) for i in range(EX...  28.5 us
    all_to_all x1, blocking collectives, per_device(): hidden = exchange(hidden, axis_index_groups=gather_groups)  24.4 us
    ppermute x7, waiting for transfers between devices, hop_along(): lax.ppermute(array, 'section', [(i, towards(i, hop, 1)) for i in range(EX...  12.6 us
    all_to_all x1, waiting for transfers between devices, per_device(): parts = exchange(parts, axis_index_groups=reduce_groups)  10.7 us
    all_to_all x1, starting transfers between devices, per_device(): parts = exchange(parts, axis_index_groups=reduce_groups)  7.53 us
    all_to_all x1, starting transfers between devices, per_device(): outputs = lax.all_to_all(outputs, 'section', 0, 0)  5.81 us
    all_to_all x1, starting transfers between devices, per_device(): down = exchange(down, axis_index_groups=reduce_groups)  4.79 us
    all_to_all x1, waiting for transfers between devices, per_device(): outputs = lax.all_to_all(outputs, 'section', 0, 0)  4.01 us
  transfers between devices with their start and end apart: 10, of which 4 were waited for; matrix products, arithmetic and copies ran while one was open for 1% of the time, Pallas kernels for 3%

profile of v1, /device:TPU:1, one launch (start us, length us, event | category | flops | bytes accessed | tf_op | source)
XLA Modules:
  0.0 113.1 jit_solution(5629293229706897769)
XLA Ops:
  0.0 0.7 broadcast_in_dim.6.gain_ref
  0.7 0.0 copy-start
  0.7 1.1 copy-done
  1.9 0.8 copy-done.4
  2.7 2.6 %shard_map.73 = (f32[8,128]{1,0:T(8,128)S(1)}, f32[8,128]{1,0:T(8,128)S(1)}, bf16[64,3072]{1,0:T(8,128)(2,1)S(1)}, bf16[64,3072]{1,0:T(8,128)(2,1)}, bf16[64,307...) custom-call(bf16[128,3072]{1,0:T(8,128)(2,1)S(1)} %bitcast.12, ...), custom_call_target="tpu_custom_call" | custom-call | tf_op jit(solution)/shard_map/pallas_call | solution.py:170
  5.3 0.8 copy-done.6
  6.0 3.9 %collective-permute-start = (bf16[64,3072]{1,0:T(8,128)(2,1)}, bf16[64,3072]{1,0:T(8,128)(2,1)}, u32[]{:S(2)}, u32[]{:S(2)}) collective-permute-start(bf16[64,3072]{1,0:T(8,128)(2,1)} %get-tuple-element.17), channel_id=1, source_target_pairs={{0,128},{64,192},{128,256},{192,320},{256,384},{320,448},{384,0},{... | collective-permute-start | bytes 1179656 | tf_op jit(solution)/shard_map/ppermute | solution.py:40
  10.0 3.2 %collective-permute-start.1 = (bf16[64,3072]{1,0:T(8,128)(2,1)}, bf16[64,3072]{1,0:T(8,128)(2,1)}, u32[]{:S(2)}, u32[]{:S(2)}) collective-permute-start(bf16[64,3072]{1,0:T(8,128)(2,1)} %get-tuple-element.18), channel_id=1, source_target_pairs={{0,384},{64,448},{128,0},{192,64},{256,128},{320,192},{384,256},{4... | collective-permute-start | bytes 1179656 | tf_op jit(solution)/shard_map/ppermute | solution.py:40
  13.2 7.1 %collective-permute-start.2 = (bf16[64,3072]{1,0:T(8,128)(2,1)}, bf16[64,3072]{1,0:T(8,128)(2,1)}, u32[]{:S(2)}, u32[]{:S(2)}) collective-permute-start(bf16[64,3072]{1,0:T(8,128)(2,1)} %get-tuple-element.19), channel_id=1, source_target_pairs={{0,192},{64,128},{128,320},{192,256},{256,448},{320,384},{384,64},... | collective-permute-start | bytes 1179656 | tf_op jit(solution)/shard_map/ppermute | solution.py:40
  20.3 3.1 %collective-permute-start.3 = (bf16[64,3072]{1,0:T(8,128)(2,1)}, bf16[64,3072]{1,0:T(8,128)(2,1)}, u32[]{:S(2)}, u32[]{:S(2)}) collective-permute-start(bf16[64,3072]{1,0:T(8,128)(2,1)} %get-tuple-element.20), channel_id=1, source_target_pairs={{0,448},{64,384},{128,64},{192,0},{256,192},{320,128},{384,320},{4... | collective-permute-start | bytes 1179656 | tf_op jit(solution)/shard_map/ppermute | solution.py:40
  23.4 5.2 %collective-permute-start.4 = (bf16[64,3072]{1,0:T(8,128)(2,1)}, bf16[64,3072]{1,0:T(8,128)(2,1)}, u32[]{:S(2)}, u32[]{:S(2)}) collective-permute-start(bf16[64,3072]{1,0:T(8,128)(2,1)} %get-tuple-element.21), channel_id=1, source_target_pairs={{0,64},{64,0},{128,192},{192,128},{256,320},{320,256},{384,448},{4... | collective-permute-start | bytes 1179656 | tf_op jit(solution)/shard_map/ppermute | solution.py:40
  28.7 1.1 shard_map.74
  29.8 4.8 %all-to-all-start = ((bf16[8,48,1024]{2,1,0:T(8,128)(2,1)}), bf16[8,48,1024]{2,1,0:T(8,128)(2,1)S(1)}, u32[]{:S(2)}, u32[]{:S(2)}) async-start(bf16[8,48,1024]{2,1,0:T(8,128)(2,1)} %shard_map.74), calls=%async_computation | async-start | bytes 1572864 | tf_op jit(solution)/shard_map/all_to_all | solution.py:180
  34.6 0.0 collective-permute-done.rest_1_
  34.6 2.2 %collective-permute-start.5 = (bf16[64,3072]{1,0:T(8,128)(2,1)S(1)}, bf16[64,3072]{1,0:T(8,128)(2,1)S(1)}, u32[]{:S(2)}, u32[]{:S(2)}) collective-permute-start(bf16[64,3072]{1,0:T(8,128)(2,1)S(1)} %get-tuple-element.22), channel_id=1, source_target_pairs={{0,256},{64,320},{128,384},{192,448},{256,0},{320,64},{384,128},{4... | collective-permute-start | bytes 1179656 | tf_op jit(solution)/shard_map/ppermute | solution.py:40
  36.8 3.6 %collective-permute-start.6 = (bf16[64,3072]{1,0:T(8,128)(2,1)S(1)}, bf16[64,3072]{1,0:T(8,128)(2,1)S(1)}, u32[]{:S(2)}, u32[]{:S(2)}) collective-permute-start(bf16[64,3072]{1,0:T(8,128)(2,1)S(1)} %get-tuple-element.23), channel_id=1, source_target_pairs={{0,320},{64,256},{128,448},{192,384},{256,64},{320,0},{384,192},{4... | collective-permute-start | bytes 1179656 | tf_op jit(solution)/shard_map/ppermute | solution.py:40
  40.5 0.0 collective-permute-done.3.rest_4_
  40.5 1.0 copy-done.7
  41.5 2.2 %shard_map.75.near_ref = bf16[384,128]{1,0:T(8,128)(2,1)S(1)} custom-call(bf16[3072,128]{1,0:T(8,128)(2,1)S(1)} %bitcast.14, bf16[3072,128]{1,0:T(8,128)(2,1)S(1)} %bitcast.16, bf16[64,3072]{1,0:T(8,128)(2,1)S(1)} %copy-done.7, bf16[64,3072]{1,0:T(8,128)(2,1)} %collective-permute-done.rest_1_, bf16[64,3072]{1,0:T(8,128)(2,1)} %collective-permute-done.1.rest_2_, ...), custom_call_target="tpu_custom_call" | custom-call | flops 17179869184 | bytes 4194304 | tf_op jit(solution)/shard_map/pallas_call | solution.py:183
  43.8 5.3 %collective-permute-done.5.rest_0_ = bf16[64,3072]{1,0:T(8,128)(2,1)S(1)} collective-permute-done((bf16[64,3072]{1,0:T(8,128)(2,1)S(1)}, bf16[64,3072]{1,0:T(8,128)(2,1)S(1)}, u32[]{:S(2)}, u32[]{:S(2)}) %collective-permute-start.5) | collective-permute-done | bytes 393248 | tf_op jit(solution)/shard_map/ppermute | solution.py:40
  49.1 7.3 %collective-permute-done.6.rest_1_ = bf16[64,3072]{1,0:T(8,128)(2,1)S(1)} collective-permute-done((bf16[64,3072]{1,0:T(8,128)(2,1)S(1)}, bf16[64,3072]{1,0:T(8,128)(2,1)S(1)}, u32[]{:S(2)}, u32[]{:S(2)}) %collective-permute-start.6) | collective-permute-done | bytes 393248 | tf_op jit(solution)/shard_map/ppermute | solution.py:40
  56.3 0.4 shard_map.76
  56.7 24.4 %all_to_all.20.hidden_ref = bf16[8,512,128]{2,1,0:T(8,128)(2,1)S(1)} all-to-all(bf16[8,512,128]{2,1,0:T(8,128)(2,1)S(1)} %shard_map.76), channel_id=1, replica_groups={{0,8,16,24,32,40,48,56},{1,9,17,25,33,41,49,57},{2,10,18,26,34,42,50,58..., dimensions={0} | all-to-all | bytes 2097152 | tf_op jit(solution)/shard_map/all_to_all | solution.py:189
  81.1 1.4 %shard_map.77 = bf16[8,48,512]{2,1,0:T(8,128)(2,1)} custom-call(bf16[8,48,1024]{2,1,0:T(8,128)(2,1)S(1)} %all-to-all-done.down_ref, bf16[8,512,128]{2,1,0:T(8,128)(2,1)S(1)} %all_to_all.20.hidden_ref), custom_call_target="tpu_custom_call" | custom-call | flops 536870912 | bytes 2097152 | tf_op jit(solution)/shard_map/pallas_call | solution.py:190
  82.5 7.5 %all-to-all-start.2 = ((bf16[8,48,512]{2,1,0:T(8,128)(2,1)}), bf16[8,48,512]{2,1,0:T(8,128)(2,1)S(1)}, u32[]{:S(2)}, u32[]{:S(2)}) async-start(bf16[8,48,512]{2,1,0:T(8,128)(2,1)} %shard_map.77), calls=%async_computation.2 | async-start | bytes 786432 | tf_op jit(solution)/shard_map/all_to_all | solution.py:191
  90.0 10.7 %all-to-all-done.2.parts_ref = bf16[8,48,512]{2,1,0:T(8,128)(2,1)S(1)} async-done(((bf16[8,48,512]{2,1,0:T(8,128)(2,1)}), bf16[8,48,512]{2,1,0:T(8,128)(2,1)S(1)}, u32[]{:S(2)}, u32[]{:S(2)}) %all-to-all-start.2) | async-done | bytes 393248 | tf_op jit(solution)/shard_map/all_to_all | solution.py:191
  100.8 0.8 shard_map.78
  101.5 5.8 %all-to-all-start.3 = ((bf16[8,48,128]{2,1,0:T(8,128)(2,1)}), bf16[8,48,128]{2,1,0:T(8,128)(2,1)S(1)}, u32[]{:S(2)}, u32[]{:S(2)}) async-start(bf16[8,48,128]{2,1,0:T(8,128)(2,1)} %shard_map.78), calls=%async_computation.3 | async-start | bytes 196608 | tf_op jit(solution)/shard_map/all_to_all | solution.py:193
  107.3 0.9 constant_dynamic-slice_fusion
  108.3 0.1 copy.8
  108.3 4.0 %all-to-all-done.3.outputs_ref = bf16[8,48,128]{2,1,0:T(8,128)(2,1)S(1)} async-done(((bf16[8,48,128]{2,1,0:T(8,128)(2,1)}), bf16[8,48,128]{2,1,0:T(8,128)(2,1)S(1)}, u32[]{:S(2)}, u32[]{:S(2)}) %all-to-all-start.3) | async-done | bytes 98336 | tf_op jit(solution)/shard_map/all_to_all | solution.py:193
  112.3 0.8 shard_map.79
  (15 shorter events, 0.0 us)
Async XLA Ops:
  0.0 0.7 copy-start.5
  0.7 1.1 %copy-start = (bf16[1,128,3072]{2,1,0:T(8,128)(2,1)S(1)}, bf16[1,128,3072]{2,1,0:T(8,128)(2,1)}, u32[]{:S(2)}) copy-start(bf16[1,128,3072]{2,1,0:T(8,128)(2,1)} %param.7) | copy-start | bytes 2359300
  1.9 0.8 copy-start.4
  2.7 26.0 %copy-start.1 = (bf16[1,48,8192]{2,1,0:T(8,128)(2,1)S(1)}, bf16[1,48,8192]{2,1,0:T(8,128)(2,1)}, u32[]{:S(2)}) copy-start(bf16[1,48,8192]{2,1,0:T(8,128)(2,1)} %param.12) | copy-start | bytes 2359300
  5.3 0.8 copy-start.6
  6.0 28.6 %collective-permute-start = (bf16[64,3072]{1,0:T(8,128)(2,1)}, bf16[64,3072]{1,0:T(8,128)(2,1)}, u32[]{:S(2)}, u32[]{:S(2)}) collective-permute-start(bf16[64,3072]{1,0:T(8,128)(2,1)} %get-tuple-element.17), channel_id=1, source_target_pairs={{0,128},{64,192},{128,256},{192,320},{256,384},{320,448},{384,0},{... | collective-permute-start | bytes 1179656 | tf_op jit(solution)/shard_map/ppermute | solution.py:40
  10.0 26.8 %collective-permute-start.1 = (bf16[64,3072]{1,0:T(8,128)(2,1)}, bf16[64,3072]{1,0:T(8,128)(2,1)}, u32[]{:S(2)}, u32[]{:S(2)}) collective-permute-start(bf16[64,3072]{1,0:T(8,128)(2,1)} %get-tuple-element.18), channel_id=1, source_target_pairs={{0,384},{64,448},{128,0},{192,64},{256,128},{320,192},{384,256},{4... | collective-permute-start | bytes 1179656 | tf_op jit(solution)/shard_map/ppermute | solution.py:40
  13.2 27.3 %collective-permute-start.2 = (bf16[64,3072]{1,0:T(8,128)(2,1)}, bf16[64,3072]{1,0:T(8,128)(2,1)}, u32[]{:S(2)}, u32[]{:S(2)}) collective-permute-start(bf16[64,3072]{1,0:T(8,128)(2,1)} %get-tuple-element.19), channel_id=1, source_target_pairs={{0,192},{64,128},{128,320},{192,256},{256,448},{320,384},{384,64},... | collective-permute-start | bytes 1179656 | tf_op jit(solution)/shard_map/ppermute | solution.py:40
  20.3 20.2 %collective-permute-start.3 = (bf16[64,3072]{1,0:T(8,128)(2,1)}, bf16[64,3072]{1,0:T(8,128)(2,1)}, u32[]{:S(2)}, u32[]{:S(2)}) collective-permute-start(bf16[64,3072]{1,0:T(8,128)(2,1)} %get-tuple-element.20), channel_id=1, source_target_pairs={{0,448},{64,384},{128,64},{192,0},{256,192},{320,128},{384,320},{4... | collective-permute-start | bytes 1179656 | tf_op jit(solution)/shard_map/ppermute | solution.py:40
  23.4 17.1 %collective-permute-start.4 = (bf16[64,3072]{1,0:T(8,128)(2,1)}, bf16[64,3072]{1,0:T(8,128)(2,1)}, u32[]{:S(2)}, u32[]{:S(2)}) collective-permute-start(bf16[64,3072]{1,0:T(8,128)(2,1)} %get-tuple-element.21), channel_id=1, source_target_pairs={{0,64},{64,0},{128,192},{192,128},{256,320},{320,256},{384,448},{4... | collective-permute-start | bytes 1179656 | tf_op jit(solution)/shard_map/ppermute | solution.py:40
  29.8 10.7 %copy-start.2 = (bf16[1,3072,128]{2,1,0:T(8,128)(2,1)S(1)}, bf16[1,3072,128]{2,1,0:T(8,128)(2,1)}, u32[]{:S(2)}) copy-start(bf16[1,3072,128]{2,1,0:T(8,128)(2,1)} %param.10) | copy-start | bytes 2359300
  29.8 10.7 %copy-start.3 = (bf16[1,3072,128]{2,1,0:T(8,128)(2,1)S(1)}, bf16[1,3072,128]{2,1,0:T(8,128)(2,1)}, u32[]{:S(2)}) copy-start(bf16[1,3072,128]{2,1,0:T(8,128)(2,1)} %param.11) | copy-start | bytes 2359300
  29.8 26.9 %all-to-all-start = ((bf16[8,48,1024]{2,1,0:T(8,128)(2,1)}), bf16[8,48,1024]{2,1,0:T(8,128)(2,1)S(1)}, u32[]{:S(2)}, u32[]{:S(2)}) async-start(bf16[8,48,1024]{2,1,0:T(8,128)(2,1)} %shard_map.74), calls=%async_computation | async-start | bytes 1572864 | tf_op jit(solution)/shard_map/all_to_all | solution.py:180
  34.6 14.5 %collective-permute-start.5 = (bf16[64,3072]{1,0:T(8,128)(2,1)S(1)}, bf16[64,3072]{1,0:T(8,128)(2,1)S(1)}, u32[]{:S(2)}, u32[]{:S(2)}) collective-permute-start(bf16[64,3072]{1,0:T(8,128)(2,1)S(1)} %get-tuple-element.22), channel_id=1, source_target_pairs={{0,256},{64,320},{128,384},{192,448},{256,0},{320,64},{384,128},{4... | collective-permute-start | bytes 1179656 | tf_op jit(solution)/shard_map/ppermute | solution.py:40
  36.8 19.5 %collective-permute-start.6 = (bf16[64,3072]{1,0:T(8,128)(2,1)S(1)}, bf16[64,3072]{1,0:T(8,128)(2,1)S(1)}, u32[]{:S(2)}, u32[]{:S(2)}) collective-permute-start(bf16[64,3072]{1,0:T(8,128)(2,1)S(1)} %get-tuple-element.23), channel_id=1, source_target_pairs={{0,320},{64,256},{128,448},{192,384},{256,64},{320,0},{384,192},{4... | collective-permute-start | bytes 1179656 | tf_op jit(solution)/shard_map/ppermute | solution.py:40
  40.5 1.0 copy-start.7
  82.5 18.3 %all-to-all-start.2 = ((bf16[8,48,512]{2,1,0:T(8,128)(2,1)}), bf16[8,48,512]{2,1,0:T(8,128)(2,1)S(1)}, u32[]{:S(2)}, u32[]{:S(2)}) async-start(bf16[8,48,512]{2,1,0:T(8,128)(2,1)} %shard_map.77), calls=%async_computation.2 | async-start | bytes 786432 | tf_op jit(solution)/shard_map/all_to_all | solution.py:191
  101.5 10.8 %all-to-all-start.3 = ((bf16[8,48,128]{2,1,0:T(8,128)(2,1)}), bf16[8,48,128]{2,1,0:T(8,128)(2,1)S(1)}, u32[]{:S(2)}, u32[]{:S(2)}) async-start(bf16[8,48,128]{2,1,0:T(8,128)(2,1)} %shard_map.78), calls=%async_computation.3 | async-start | bytes 196608 | tf_op jit(solution)/shard_map/all_to_all | solution.py:193

commit v2 on v1

v2 whole, which is shorter than its diff:
```python
import functools

import jax
import jax.numpy as jnp
from jax import lax
from jax.experimental import pallas as pl
from jax.experimental.pallas import tpu as pltpu
from jax.sharding import PartitionSpec as P

CAP = 64
CHIPS = 4
RING = 8
EXPERTS = 2 * CHIPS
HOPS = ((0, 0), (1, 0), (3, 0), (1, 1), (0, 1), (3, 1), (2, 0), (2, 1))
NEAR = 5
NEAR_FLOPS, FAR_FLOPS = 2**34, 2**28
PIECES = 4
FULL = 60
AXES = ("section", "expert")
bf16, f32 = jnp.bfloat16, jnp.float32


def params(mib):
    return pltpu.CompilerParams(vmem_limit_bytes=mib * 2**20)


def call(kernel, out_shape, mib, flops=0, nbytes=0):
    return pl.pallas_call(
        kernel,
        out_shape=out_shape,
        compiler_params=params(mib),
        cost_estimate=pl.CostEstimate(flops=flops, bytes_accessed=nbytes, transcendentals=0),
    )


def towards(section, hop, sign):
    x, core = section // 2, section % 2
    return 2 * ((x + sign * hop[0]) % CHIPS) + (core + hop[1]) % 2


def hop_along(array, hop):
    return lax.ppermute(array, "section", [(i, towards(i, hop, 1)) for i in range(EXPERTS)])


def ring_groups():
    def place(section, z, y):
        return section * RING * RING + z * RING + y

    gather, reduce, wide = [], [], []
    for core in range(2):
        for u in range(RING):
            by_z = [[place(2 * x + core, v, u) for v in range(RING)] for x in range(CHIPS)]
            by_y = [[place(2 * x + core, u, v) for v in range(RING)] for x in range(CHIPS)]
            gather += by_y if core else by_z
            across = by_z if core else by_y
            reduce += across
            wide.append([device for line in across for device in line])
    return gather, reduce, wide


def norm_rows(tok_ref, gain_ref):
    x = tok_ref[...].astype(f32)
    mean_sq = jnp.mean(x * x, axis=-1, keepdims=True)
    return (x * lax.rsqrt(mean_sq + 1e-05) * gain_ref[...].astype(f32)).astype(bf16)


def ranks_of(ids):
    rows = ids.shape[1]
    labels = lax.broadcasted_iota(jnp.int32, (EXPERTS, rows), 0)
    chosen = jnp.where((labels == ids[0:1]) | (labels == ids[1:2]), 1.0, 0.0)
    tall = lax.broadcasted_iota(jnp.int32, (rows, rows), 0)
    wide = lax.broadcasted_iota(jnp.int32, (rows, rows), 1)
    upto = jnp.where(tall <= wide, 1.0, 0.0).astype(bf16)
    ranks = jnp.dot(chosen.astype(bf16), upto, preferred_element_type=f32)
    return jnp.where(chosen > 0.0, ranks - 1.0, -1.0)


def placing_of(rank_row):
    slots = lax.broadcasted_iota(jnp.int32, (CAP, rank_row.shape[1]), 0).astype(f32)
    return jnp.where(slots == rank_row, 1.0, 0.0)


def pack_kernel(tok_ref, gain_ref, routing_ref, *rest):
    packed_refs, rank_ref = rest[:-1], rest[-1]
    section = lax.axis_index("section")
    rank_ref[...] = ranks_of(routing_ref[section])
    placing = jnp.concatenate(
        [placing_of(rank_ref[pl.ds(towards(section, hop, 1), 1), :]) for hop in HOPS[1:]], axis=0
    ).astype(bf16)
    normed = norm_rows(tok_ref, gain_ref)
    packed = jnp.dot(placing, normed, preferred_element_type=f32).astype(bf16)
    for k, ref in enumerate(packed_refs):
        ref[...] = packed[k * CAP : (k + 1) * CAP]


def share_kernel(tok_ref, gain_ref, routing_ref, router_ref, weight_ref, rank_ref, own_ref):
    section = lax.axis_index("section")
    ids = routing_ref[section]
    rank_ref[...] = ranks_of(ids)
    normed = norm_rows(tok_ref, gain_ref)
    placing = placing_of(rank_ref[pl.ds(section, 1), :]).astype(bf16)
    own_ref[...] = jnp.dot(placing, normed, preferred_element_type=f32).astype(bf16)
    logits = lax.dot_general(
        router_ref[...], normed, (((1,), (1,)), ((), ())), preferred_element_type=f32
    )
    labels = lax.broadcasted_iota(jnp.int32, logits.shape, 0)
    is_first, is_second = labels == ids[0:1], labels == ids[1:2]
    margin = jnp.sum(jnp.where(is_first, logits, 0.0), axis=0, keepdims=True) - jnp.sum(
        jnp.where(is_second, logits, 0.0), axis=0, keepdims=True
    )
    weight_ref[...] = jnp.where(
        is_first, jax.nn.sigmoid(margin), jnp.where(is_second, jax.nn.sigmoid(-margin), 0.0)
    )


def regroup_kernel(down_ref, out_ref):
    swap = lax.axis_index("section") % 2
    major, minor = jnp.where(swap == 1, RING, 1), jnp.where(swap == 1, 1, RING)
    for p in range(RING):
        for q in range(RING):
            at = pl.multiple_of((p * major + q * minor) * 128, 128)
            out_ref[p, :, q * 128 : (q + 1) * 128] = down_ref[:, pl.ds(at, 128)]


def hidden_rows(gate, up, block_refs, gate_ref, up_ref, rows_ref, sems):
    depth, width = gate_ref.shape
    piece = depth // PIECES

    def copies(at):
        span = pl.ds(at * piece, piece)
        pairs = [(gate.at[span], gate_ref.at[span]), (up.at[span], up_ref.at[span])] + [
            (ref.at[:, span], rows_ref.at[pl.ds(k * CAP, CAP), span])
            for k, ref in enumerate(block_refs)
        ]
        return [
            pltpu.make_async_copy(source, target, sems.at[at, k])
            for k, (source, target) in enumerate(pairs)
        ]

    landing = [copies(at) for at in range(PIECES)]
    for group in landing:
        for copy in group:
            copy.start()
    total = None
    for at, group in enumerate(landing):
        for copy in group:
            copy.wait()
        for k in range(at * piece, (at + 1) * piece, 256):
            right = jnp.concatenate([gate_ref[k : k + 256], up_ref[k : k + 256]], axis=1)
            term = jnp.dot(rows_ref[:, k : k + 256], right, preferred_element_type=f32)
            total = term if total is None else total + term
    return (jax.nn.silu(total[:, :width]) * total[:, width:]).astype(bf16)


def hidden_kernel(first, gate, up, *rest):
    *block_refs, out_ref, gate_ref, up_ref, rows_ref, made_ref, sems, out_sems = rest
    if first:
        block_refs = block_refs[1:]
    made_ref[...] = hidden_rows(gate, up, block_refs, gate_ref, up_ref, rows_ref, sems)
    copies = [
        pltpu.make_async_copy(
            made_ref, out_ref.at[p, pl.ds(first, made_ref.shape[0])], out_sems.at[p]
        )
        for p in range(RING)
    ]
    for copy in copies:
        copy.start()
    for copy in copies:
        copy.wait()


def project_kernel(down_ref, hidden_ref, out_ref):
    blocks, cols, depth = down_ref.shape
    width = hidden_ref.shape[2]
    total = None
    for q in range(0, RING, 2):
        left = down_ref[:, :, q * width : (q + 2) * width].reshape(blocks * cols, 2 * width)
        right = jnp.concatenate([hidden_ref[q], hidden_ref[q + 1]], axis=1)
        term = lax.dot_general(left, right, (((1,), (1,)), ((), ())), preferred_element_type=f32)
        total = term if total is None else total + term
    parts = total.astype(bf16).reshape(blocks, cols, -1)
    x = lax.axis_index("section") // 2
    for steps in range(CHIPS):
        same, other = HOPS.index((steps, 0)) * CAP, HOPS.index((steps, 1)) * CAP
        pair = [parts[:, :, same : same + CAP], parts[:, :, other : other + CAP]]
        out_ref[pl.ds((x + CHIPS - steps) % CHIPS * RING, RING)] = jnp.concatenate(pair, axis=2)


def sum_kernel(parts_ref, out_ref):
    for x in range(CHIPS):
        total = jnp.sum(parts_ref[x * RING : (x + 1) * RING].astype(f32), axis=0)
        out_ref[x] = total.astype(bf16)


def combine_kernel(mine_ref, theirs_ref, weight_ref, rank_ref, own_ref, out_ref):
    rows = own_ref.shape[1]
    core = lax.axis_index("section") % 2
    slots = lax.broadcasted_iota(jnp.int32, (CAP, rows), 0).astype(f32)
    total = own_ref[...].astype(f32)
    for x in range(CHIPS):
        for ref, at, parity in ((mine_ref, 0, core), (theirs_ref, CAP, 1 - core)):
            row = pl.ds(2 * x + parity, 1)
            placing = jnp.where(slots == rank_ref[row, :], 1.0, 0.0).astype(bf16)
            picked = jnp.dot(ref[x, :, at : at + CAP], placing, preferred_element_type=f32)
            total = total + weight_ref[row, :] * picked
    out_ref[...] = total.astype(bf16)


def hidden_of(gate, up, slots, flops, first, before, blocks):
    depth, width = gate.shape
    operands = [gate, up, *before, *blocks]
    return pl.pallas_call(
        functools.partial(hidden_kernel, first),
        out_shape=jax.ShapeDtypeStruct((RING, slots, width), bf16),
        in_specs=[pl.BlockSpec(memory_space=pl.ANY)] * len(operands),
        out_specs=pl.BlockSpec(memory_space=pl.ANY),
        scratch_shapes=[
            pltpu.VMEM(gate.shape, bf16),
            pltpu.VMEM(gate.shape, bf16),
            pltpu.VMEM((len(blocks) * CAP, depth), bf16),
            pltpu.VMEM((len(blocks) * CAP, width), bf16),
            pltpu.SemaphoreType.DMA((PIECES, 2 + len(blocks))),
            pltpu.SemaphoreType.DMA((RING,)),
        ],
        input_output_aliases={2: 0} if before else {},
        compiler_params=params(FULL),
        cost_estimate=pl.CostEstimate(flops=flops, bytes_accessed=2**22, transcendentals=0),
    )(*operands)


def per_device(tokens, gains, w_router, w_gate, w_up, w_down, routing):
    gather_groups, reduce_groups, wide_groups = ring_groups()
    exchange = functools.partial(
        lax.all_to_all, axis_name=AXES, split_axis=0, concat_axis=0
    )
    rows, depth = tokens.shape[1:]
    width, cols = w_gate.shape[2], w_down.shape[1]
    shape = jax.ShapeDtypeStruct
    block = shape((CAP, depth), bf16)

    ids = jnp.swapaxes(routing, 1, 2)
    packed = pl.pallas_call(
        pack_kernel,
        out_shape=[block] * (len(HOPS) - 1),
        scratch_shapes=[pltpu.VMEM((EXPERTS, rows), f32)],
        compiler_params=params(12),
    )(tokens[0], gains, ids)
    arrived = [hop_along(array, hop) for array, hop in zip(packed, HOPS[1:], strict=True)]
    late_tokens, _ = lax.optimization_barrier((tokens[0], arrived[0]))
    late_down, *_ = lax.optimization_barrier((w_down[0], *arrived[:3]))
    weight, rank, own = pl.pallas_call(
        share_kernel,
        out_shape=[shape((EXPERTS, rows), f32)] * 2 + [block],
        compiler_params=params(12),
    )(late_tokens, gains, ids, w_router.T)
    down = call(regroup_kernel, shape((RING, cols, RING * width), bf16), 8)(late_down)
    down = exchange(down, axis_index_groups=reduce_groups)

    slots = len(HOPS) * CAP
    near, far = [own] + arrived[: NEAR - 1], arrived[NEAR - 1 :]
    hidden_call = functools.partial(hidden_of, w_gate[0], w_up[0], slots)
    hidden = hidden_call(NEAR_FLOPS, 0, [], near)
    hidden = hidden_call(FAR_FLOPS, NEAR * CAP, [hidden], far)
    hidden = exchange(hidden, axis_index_groups=gather_groups)
    pair = (CHIPS * RING, cols, 2 * CAP)
    parts = call(project_kernel, shape(pair, bf16), 16, 2**29, 2**21)(down, hidden)
    parts = exchange(parts, axis_index_groups=wide_groups)
    mine = call(sum_kernel, shape((CHIPS, cols, 2 * CAP), bf16), 8)(parts)
    theirs = hop_along(mine, (0, 1))
    own = lax.dynamic_slice_in_dim(tokens[0], lax.axis_index("expert") * cols, cols, 1)
    result = call(combine_kernel, shape((cols, rows), bf16), 8)(mine, theirs, weight, rank, own.T)
    return result.T[None]


def solution(mesh):
    in_specs = (
        P("section", None, None),
        P(),
        P(),
        P("section", None, "expert"),
        P("section", None, "expert"),
        P("section", "expert", None),
        P(),
    )
    out_specs = P("section", None, "expert")
    return jax.shard_map(
        per_device, mesh=mesh, in_specs=in_specs, out_specs=out_specs, check_vma=False
    )
```

time: 114 us -> 108 us (0.947)
  waiting for transfers between devices: 27.3 us -> 17.7 us
  Pallas kernels: 9.27 us -> 12.3 us
  local copies, waits for them, and re-layouts: 5.39 us -> 4.17 us
    ppermute x7 -> x8, starting transfers between devices: 28.5 us -> 34.5 us  [hop_along(): lax.ppermute(array, 'section', [(i, towards(i, hop, 1)) for i in range(EX...]
    ppermute x7 -> x8, waiting for transfers between devices: 12.6 us -> 7.2 us  [hop_along(): lax.ppermute(array, 'section', [(i, towards(i, hop, 1)) for i in range(EX...]
    all_to_all x2 -> x1, starting transfers between devices: 13.3 us -> 8.38 us  [per_device(): parts = exchange(parts, axis_index_groups=wide_groups)]
    all_to_all x2 -> x1, waiting for transfers between devices: 14.7 us -> 10.5 us  [per_device(): parts = exchange(parts, axis_index_groups=wide_groups)]
    pallas_call x6 -> x7, Pallas kernels: 8.47 us -> 11.5 us  [the longest x2 7.04 us: hidden_of(): pl.pallas_call(functools.partial(hidden_kernel, first), out_shape=jax.Sha...]
    unnamed x16 -> x24, local copies, waits for them, and re-layouts: 3.69 us -> 4 us
  transfers between devices with their start and end apart: 10 -> 10, of which waited for: 4 -> 3; matrix products, arithmetic and copies ran while one was open for 1% -> 0% of each run, Pallas kernels for 3% -> 8%
where the time goes in v2:
time: 108 us; the launch traced here: 107 us
  starting transfers between devices  47.7 us (44%)
  blocking collectives  24.5 us (23%)
  waiting for transfers between devices  17.7 us (16%)
  Pallas kernels  12.3 us (11%)
  local copies, waits for them, and re-layouts  4.17 us (4%)
    ppermute x8, starting transfers between devices, hop_along(): lax.ppermute(array, 'section', [(i, towards(i, hop, 1)) for i in range(EX...  34.5 us
    all_to_all x1, blocking collectives, per_device(): hidden = exchange(hidden, axis_index_groups=gather_groups)  24.5 us
    all_to_all x1, waiting for transfers between devices, per_device(): parts = exchange(parts, axis_index_groups=wide_groups)  10.5 us
    all_to_all x1, starting transfers between devices, per_device(): parts = exchange(parts, axis_index_groups=wide_groups)  8.38 us
    ppermute x8, waiting for transfers between devices, hop_along(): lax.ppermute(array, 'section', [(i, towards(i, hop, 1)) for i in range(EX...  7.2 us
    pallas_call x2, Pallas kernels, hidden_of(): pl.pallas_call(functools.partial(hidden_kernel, first), out_shape=jax.Sha...  7.04 us
    all_to_all x1, starting transfers between devices, per_device(): down = exchange(down, axis_index_groups=reduce_groups)  4.81 us
    unnamed x24, local copies, waits for them, and re-layouts  4 us
  transfers between devices with their start and end apart: 10, of which 3 were waited for; matrix products, arithmetic and copies ran while one was open for 0% of the time, Pallas kernels for 8%

profile of v2, /device:TPU:1, one launch (start us, length us, event | category | flops | bytes accessed | tf_op | source)
XLA Modules:
  0.0 106.6 jit_solution(2839987945815563255)
XLA Ops:
  0.0 1.1 %copy-done = bf16[1,128,3072]{2,1,0:T(8,128)(2,1)S(1)} copy-done((bf16[1,128,3072]{2,1,0:T(8,128)(2,1)S(1)}, bf16[1,128,3072]{2,1,0:T(8,128)(2,1)}, u32[]{:S(2)}) %copy-start) | copy-done | bytes 786456
  1.1 0.7 copy-done.4
  1.8 0.7 copy-done.6
  2.5 1.1 %shard_map.73 = (bf16[64,3072]{1,0:T(8,128)(2,1)S(1)}, bf16[64,3072]{1,0:T(8,128)(2,1)S(1)}, bf16[64,3072]{1,0:T(8,128)(2,1)S(1)}, bf16[64,3072]{1,0:T(8,128)(2,...) custom-call(bf16[128,3072]{1,0:T(8,128)(2,1)S(1)} %bitcast.12, ...), custom_call_target="tpu_custom_call" | custom-call | tf_op jit(solution)/shard_map/pallas_call | solution.py:242
  3.6 4.0 %collective-permute-start = (bf16[64,3072]{1,0:T(8,128)(2,1)S(1)}, bf16[64,3072]{1,0:T(8,128)(2,1)S(1)}, u32[]{:S(2)}, u32[]{:S(2)}) collective-permute-start(bf16[64,3072]{1,0:T(8,128)(2,1)S(1)} %get-tuple-element.17), channel_id=1, source_target_pairs={{0,128},{64,192},{128,256},{192,320},{256,384},{320,448},{384,0},{... | collective-permute-start | bytes 1179656 | tf_op jit(solution)/shard_map/ppermute | solution.py:42
  7.6 3.2 %collective-permute-start.1 = (bf16[64,3072]{1,0:T(8,128)(2,1)S(1)}, bf16[64,3072]{1,0:T(8,128)(2,1)S(1)}, u32[]{:S(2)}, u32[]{:S(2)}) collective-permute-start(bf16[64,3072]{1,0:T(8,128)(2,1)S(1)} %get-tuple-element.18), channel_id=1, source_target_pairs={{0,384},{64,448},{128,0},{192,64},{256,128},{320,192},{384,256},{4... | collective-permute-start | bytes 1179656 | tf_op jit(solution)/shard_map/ppermute | solution.py:42
  10.8 7.1 %collective-permute-start.2 = (bf16[64,3072]{1,0:T(8,128)(2,1)S(1)}, bf16[64,3072]{1,0:T(8,128)(2,1)S(1)}, u32[]{:S(2)}, u32[]{:S(2)}) collective-permute-start(bf16[64,3072]{1,0:T(8,128)(2,1)S(1)} %get-tuple-element.19), channel_id=1, source_target_pairs={{0,192},{64,128},{128,320},{192,256},{256,448},{320,384},{384,64},... | collective-permute-start | bytes 1179656 | tf_op jit(solution)/shard_map/ppermute | solution.py:42
  17.9 3.5 %collective-permute-start.3 = (bf16[64,3072]{1,0:T(8,128)(2,1)S(1)}, bf16[64,3072]{1,0:T(8,128)(2,1)}, u32[]{:S(2)}, u32[]{:S(2)}) collective-permute-start(bf16[64,3072]{1,0:T(8,128)(2,1)S(1)} %get-tuple-element.23), channel_id=1, source_target_pairs={{0,64},{64,0},{128,192},{192,128},{256,320},{320,256},{384,448},{4... | collective-permute-start | bytes 1179656 | tf_op jit(solution)/shard_map/ppermute | solution.py:42
  21.4 4.9 %collective-permute-start.4 = (bf16[64,3072]{1,0:T(8,128)(2,1)S(1)}, bf16[64,3072]{1,0:T(8,128)(2,1)}, u32[]{:S(2)}, u32[]{:S(2)}) collective-permute-start(bf16[64,3072]{1,0:T(8,128)(2,1)S(1)} %get-tuple-element.24), channel_id=1, source_target_pairs={{0,448},{64,384},{128,64},{192,0},{256,192},{320,128},{384,320},{4... | collective-permute-start | bytes 1179656 | tf_op jit(solution)/shard_map/ppermute | solution.py:42
  26.3 0.0 collective-permute-done.rest_1_
  26.3 1.9 %collective-permute-start.5 = (bf16[64,3072]{1,0:T(8,128)(2,1)S(1)}, bf16[64,3072]{1,0:T(8,128)(2,1)}, u32[]{:S(2)}, u32[]{:S(2)}) collective-permute-start(bf16[64,3072]{1,0:T(8,128)(2,1)S(1)} %get-tuple-element.25), channel_id=1, source_target_pairs={{0,256},{64,320},{128,384},{192,448},{256,0},{320,64},{384,128},{4... | collective-permute-start | bytes 1179656 | tf_op jit(solution)/shard_map/ppermute | solution.py:42
  28.2 0.0 collective-permute-done.1.rest_2_
  28.3 5.0 %collective-permute-start.6 = (bf16[64,3072]{1,0:T(8,128)(2,1)S(1)}, bf16[64,3072]{1,0:T(8,128)(2,1)}, u32[]{:S(2)}, u32[]{:S(2)}) collective-permute-start(bf16[64,3072]{1,0:T(8,128)(2,1)S(1)} %get-tuple-element.26), channel_id=1, source_target_pairs={{0,320},{64,256},{128,448},{192,384},{256,64},{320,0},{384,192},{4... | collective-permute-start | bytes 1179656 | tf_op jit(solution)/shard_map/ppermute | solution.py:42
  33.4 0.7 copy-done.11
  34.1 1.1 %shard_map.74 = bf16[8,48,1024]{2,1,0:T(8,128)(2,1)} custom-call(bf16[48,8192]{1,0:T(8,128)(2,1)S(1)} %bitcast.14), custom_call_target="tpu_custom_call" | custom-call | tf_op jit(solution)/shard_map/pallas_call | solution.py:256
  35.2 4.8 %all-to-all-start = ((bf16[8,48,1024]{2,1,0:T(8,128)(2,1)}), bf16[8,48,1024]{2,1,0:T(8,128)(2,1)S(1)}, u32[]{:S(2)}, u32[]{:S(2)}) async-start(bf16[8,48,1024]{2,1,0:T(8,128)(2,1)} %shard_map.74), calls=%async_computation | async-start | bytes 1572864 | tf_op jit(solution)/shard_map/all_to_all | solution.py:257
  40.0 0.7 shard_map.75
  40.8 0.7 copy-done.8
  41.5 0.0 collective-permute-done.3.rest_4_
  41.5 3.9 %shard_map.76.rest_0_ = bf16[8,512,128]{2,1,0:T(8,128)(2,1)} custom-call(bf16[3072,128]{1,0:T(8,128)(2,1)} %bitcast.19, bf16[3072,128]{1,0:T(8,128)(2,1)} %bitcast.21, bf16[64,3072]{1,0:T(8,128)(2,1)} %copy-done.8, bf16[64,3072]{1,0:T(8,128)(2,1)} %copy-done.9, bf16[64,3072]{1,0:T(8,128)(2,1)} %copy-done.10, bf16[64,3072]{1,0:T(8,128)(2,1)} %copy-done.11, ...), custom_call_target="tpu_custom_call" | custom-call | flops 17179869184 | bytes 4194304 | tf_op jit(solution)/shard_map/pallas_call | solution.py:212
  45.4 6.5 %collective-permute-done.4.rest_1_ = bf16[64,3072]{1,0:T(8,128)(2,1)} collective-permute-done((bf16[64,3072]{1,0:T(8,128)(2,1)S(1)}, bf16[64,3072]{1,0:T(8,128)(2,1)}, u32[]{:S(2)}, u32[]{:S(2)}) %collective-permute-start.4) | collective-permute-done | bytes 393248 | tf_op jit(solution)/shard_map/ppermute | solution.py:42
  51.9 3.2 %shard_map.77 = bf16[8,512,128]{2,1,0:T(8,128)(2,1)} custom-call(bf16[3072,128]{1,0:T(8,128)(2,1)} %bitcast.20, bf16[3072,128]{1,0:T(8,128)(2,1)} %bitcast.22, bf16[8,512,128]{2,1,0:T(8,128)(2,1)} %shard_map.76.rest_0_, bf16[64,3072]{1,0:T(8,128)(2,1)} %collective-permute-done.4.rest_1_, ...), custom_call_target="tpu_custom_call", output_to_operand_aliasing={{}: (2, {})} | custom-call | flops 268435456 | bytes 4194304 | tf_op jit(solution)/shard_map/pallas_call | solution.py:212
  55.1 24.5 %all_to_all.15.hidden_ref = bf16[8,512,128]{2,1,0:T(8,128)(2,1)S(1)} all-to-all(bf16[8,512,128]{2,1,0:T(8,128)(2,1)} %shard_map.77), channel_id=1, replica_groups={{0,8,16,24,32,40,48,56},{128,136,144,152,160,168,176,184},{256,264,272,..., dimensions={0} | all-to-all | bytes 2097152 | tf_op jit(solution)/shard_map/all_to_all | solution.py:264
  79.6 1.4 %shard_map.78 = bf16[32,48,128]{2,1,0:T(8,128)(2,1)} custom-call(bf16[8,48,1024]{2,1,0:T(8,128)(2,1)S(1)} %all-to-all-done.down_ref, bf16[8,512,128]{2,1,0:T(8,128)(2,1)S(1)} %all_to_all.15.hidden_ref), custom_call_target="tpu_custom_call" | custom-call | flops 536870912 | bytes 2097152 | tf_op jit(solution)/shard_map/pallas_call | solution.py:266
  81.0 8.4 %all-to-all-start.2 = ((bf16[32,48,128]{2,1,0:T(8,128)(2,1)}), bf16[32,48,128]{2,1,0:T(8,128)(2,1)S(1)}, u32[]{:S(2)}, u32[]{:S(2)}) async-start(bf16[32,48,128]{2,1,0:T(8,128)(2,1)} %shard_map.78), calls=%async_computation.2 | async-start | bytes 786432 | tf_op jit(solution)/shard_map/all_to_all | solution.py:267
  89.4 10.5 %all-to-all-done.2.parts_ref = bf16[32,48,128]{2,1,0:T(8,128)(2,1)S(1)} async-done(((bf16[32,48,128]{2,1,0:T(8,128)(2,1)}), bf16[32,48,128]{2,1,0:T(8,128)(2,1)S(1)}, u32[]{:S(2)}, u32[]{:S(2)}) %all-to-all-start.2) | async-done | bytes 393248 | tf_op jit(solution)/shard_map/all_to_all | solution.py:267
  99.9 0.1 shard_map.79.mine_ref
  100.0 4.9 %collective-permute-start.7 = (bf16[4,48,128]{2,1,0:T(8,128)(2,1)S(1)}, bf16[4,48,128]{2,1,0:T(8,128)(2,1)S(1)}, u32[]{:S(2)}, u32[]{:S(2)}) collective-permute-start(bf16[4,48,128]{2,1,0:T(8,128)(2,1)S(1)} %shard_map.79.mine_ref), channel_id=1, source_target_pairs={{0,64},{64,0},{128,192},{192,128},{256,320},{320,256},{384,448},{4... | collective-permute-start | bytes 147464 | tf_op jit(solution)/shard_map/ppermute | solution.py:42
  104.9 0.1 constant_dynamic-slice_fusion
  105.0 0.1 copy.9
  105.1 0.7 collective-permute-done.7.theirs_ref
  105.7 0.8 shard_map.80
  (23 shorter events, 0.0 us)
Async XLA Ops:
  0.0 1.1 %copy-start = (bf16[1,128,3072]{2,1,0:T(8,128)(2,1)S(1)}, bf16[1,128,3072]{2,1,0:T(8,128)(2,1)}, u32[]{:S(2)}) copy-start(bf16[1,128,3072]{2,1,0:T(8,128)(2,1)} %param.7) | copy-start | bytes 2359300
  1.1 0.7 copy-start.4
  1.8 0.7 copy-start.6
  2.5 31.6 %copy-start.2 = (bf16[1,48,8192]{2,1,0:T(8,128)(2,1)S(1)}, bf16[1,48,8192]{2,1,0:T(8,128)(2,1)}, u32[]{:S(2)}) copy-start(bf16[1,48,8192]{2,1,0:T(8,128)(2,1)} %param.12) | copy-start | bytes 2359300
  3.6 22.7 %collective-permute-start = (bf16[64,3072]{1,0:T(8,128)(2,1)S(1)}, bf16[64,3072]{1,0:T(8,128)(2,1)S(1)}, u32[]{:S(2)}, u32[]{:S(2)}) collective-permute-start(bf16[64,3072]{1,0:T(8,128)(2,1)S(1)} %get-tuple-element.17), channel_id=1, source_target_pairs={{0,128},{64,192},{128,256},{192,320},{256,384},{320,448},{384,0},{... | collective-permute-start | bytes 1179656 | tf_op jit(solution)/shard_map/ppermute | solution.py:42
  7.6 20.7 %collective-permute-start.1 = (bf16[64,3072]{1,0:T(8,128)(2,1)S(1)}, bf16[64,3072]{1,0:T(8,128)(2,1)S(1)}, u32[]{:S(2)}, u32[]{:S(2)}) collective-permute-start(bf16[64,3072]{1,0:T(8,128)(2,1)S(1)} %get-tuple-element.18), channel_id=1, source_target_pairs={{0,384},{64,448},{128,0},{192,64},{256,128},{320,192},{384,256},{4... | collective-permute-start | bytes 1179656 | tf_op jit(solution)/shard_map/ppermute | solution.py:42
  10.8 22.5 %collective-permute-start.2 = (bf16[64,3072]{1,0:T(8,128)(2,1)S(1)}, bf16[64,3072]{1,0:T(8,128)(2,1)S(1)}, u32[]{:S(2)}, u32[]{:S(2)}) collective-permute-start(bf16[64,3072]{1,0:T(8,128)(2,1)S(1)} %get-tuple-element.19), channel_id=1, source_target_pairs={{0,192},{64,128},{128,320},{192,256},{256,448},{320,384},{384,64},... | collective-permute-start | bytes 1179656 | tf_op jit(solution)/shard_map/ppermute | solution.py:42
  17.9 23.6 %collective-permute-start.3 = (bf16[64,3072]{1,0:T(8,128)(2,1)S(1)}, bf16[64,3072]{1,0:T(8,128)(2,1)}, u32[]{:S(2)}, u32[]{:S(2)}) collective-permute-start(bf16[64,3072]{1,0:T(8,128)(2,1)S(1)} %get-tuple-element.23), channel_id=1, source_target_pairs={{0,64},{64,0},{128,192},{192,128},{256,320},{320,256},{384,448},{4... | collective-permute-start | bytes 1179656 | tf_op jit(solution)/shard_map/ppermute | solution.py:42
  21.4 30.4 %collective-permute-start.4 = (bf16[64,3072]{1,0:T(8,128)(2,1)S(1)}, bf16[64,3072]{1,0:T(8,128)(2,1)}, u32[]{:S(2)}, u32[]{:S(2)}) collective-permute-start(bf16[64,3072]{1,0:T(8,128)(2,1)S(1)} %get-tuple-element.24), channel_id=1, source_target_pairs={{0,448},{64,384},{128,64},{192,0},{256,192},{320,128},{384,320},{4... | collective-permute-start | bytes 1179656 | tf_op jit(solution)/shard_map/ppermute | solution.py:42
  26.3 7.0 %copy-start.9 = (bf16[64,3072]{1,0:T(8,128)(2,1)}, bf16[64,3072]{1,0:T(8,128)(2,1)S(1)}, u32[]{:S(2)}) copy-start(bf16[64,3072]{1,0:T(8,128)(2,1)S(1)} %collective-permute-done.rest_1_) | copy-start | bytes 1179652
  26.3 25.6 %collective-permute-start.5 = (bf16[64,3072]{1,0:T(8,128)(2,1)S(1)}, bf16[64,3072]{1,0:T(8,128)(2,1)}, u32[]{:S(2)}, u32[]{:S(2)}) collective-permute-start(bf16[64,3072]{1,0:T(8,128)(2,1)S(1)} %get-tuple-element.25), channel_id=1, source_target_pairs={{0,256},{64,320},{128,384},{192,448},{256,0},{320,64},{384,128},{4... | collective-permute-start | bytes 1179656 | tf_op jit(solution)/shard_map/ppermute | solution.py:42
  28.3 5.1 %copy-start.10 = (bf16[64,3072]{1,0:T(8,128)(2,1)}, bf16[64,3072]{1,0:T(8,128)(2,1)S(1)}, u32[]{:S(2)}) copy-start(bf16[64,3072]{1,0:T(8,128)(2,1)S(1)} %collective-permute-done.1.rest_2_) | copy-start | bytes 1179652
  28.3 23.6 %collective-permute-start.6 = (bf16[64,3072]{1,0:T(8,128)(2,1)S(1)}, bf16[64,3072]{1,0:T(8,128)(2,1)}, u32[]{:S(2)}, u32[]{:S(2)}) collective-permute-start(bf16[64,3072]{1,0:T(8,128)(2,1)S(1)} %get-tuple-element.26), channel_id=1, source_target_pairs={{0,320},{64,256},{128,448},{192,384},{256,64},{320,0},{384,192},{4... | collective-permute-start | bytes 1179656 | tf_op jit(solution)/shard_map/ppermute | solution.py:42
  33.3 0.7 copy-start.11
  35.2 4.8 %copy-start.1 = (bf16[1,128,3072]{2,1,0:T(8,128)(2,1)S(1)}, bf16[1,128,3072]{2,1,0:T(8,128)(2,1)}, u32[]{:S(2)}) copy-start(bf16[1,128,3072]{2,1,0:T(8,128)(2,1)} %param.7) | copy-start | bytes 2359300
  35.2 4.8 %copy-start.3 = (bf16[3072,8]{0,1:T(8,128)(2,1)S(1)}, bf16[3072,8]{0,1:T(8,128)(2,1)}, u32[]{:S(2)}) copy-start(bf16[3072,8]{0,1:T(8,128)(2,1)} %param.9) | copy-start | bytes 147460
  35.2 4.8 %copy-start.5 = (s32[8,128,2]{1,2,0:T(2,128)S(1)}, s32[8,128,2]{1,2,0:T(2,128)}, u32[]{:S(2)}) copy-start(s32[8,128,2]{1,2,0:T(2,128)} %param.13) | copy-start | bytes 24580
  35.2 4.8 %copy-start.7 = (bf16[3072]{0:T(1024)(128)(2,1)S(1)}, bf16[3072]{0:T(1024)(128)(2,1)}, u32[]{:S(2)}) copy-start(bf16[3072]{0:T(1024)(128)(2,1)} %gain_ref.3) | copy-start | bytes 18436
  35.2 19.9 %all-to-all-start = ((bf16[8,48,1024]{2,1,0:T(8,128)(2,1)}), bf16[8,48,1024]{2,1,0:T(8,128)(2,1)S(1)}, u32[]{:S(2)}, u32[]{:S(2)}) async-start(bf16[8,48,1024]{2,1,0:T(8,128)(2,1)} %shard_map.74), calls=%async_computation | async-start | bytes 1572864 | tf_op jit(solution)/shard_map/all_to_all | solution.py:257
  40.8 0.7 copy-start.8
  81.0 18.9 %all-to-all-start.2 = ((bf16[32,48,128]{2,1,0:T(8,128)(2,1)}), bf16[32,48,128]{2,1,0:T(8,128)(2,1)S(1)}, u32[]{:S(2)}, u32[]{:S(2)}) async-start(bf16[32,48,128]{2,1,0:T(8,128)(2,1)} %shard_map.78), calls=%async_computation.2 | async-start | bytes 786432 | tf_op jit(solution)/shard_map/all_to_all | solution.py:267
  100.0 5.8 %collective-permute-start.7 = (bf16[4,48,128]{2,1,0:T(8,128)(2,1)S(1)}, bf16[4,48,128]{2,1,0:T(8,128)(2,1)S(1)}, u32[]{:S(2)}, u32[]{:S(2)}) collective-permute-start(bf16[4,48,128]{2,1,0:T(8,128)(2,1)S(1)} %shard_map.79.mine_ref), channel_id=1, source_target_pairs={{0,64},{64,0},{128,192},{192,128},{256,320},{320,256},{384,448},{4... | collective-permute-start | bytes 147464 | tf_op jit(solution)/shard_map/ppermute | solution.py:42

commit v3 on v2

--- a/solution.py
+++ b/solution.py
@@ -14,7 +14,7 @@
 HOPS = ((0, 0), (1, 0), (3, 0), (1, 1), (0, 1), (3, 1), (2, 0), (2, 1))
 NEAR = 5
 NEAR_FLOPS, FAR_FLOPS = 2**34, 2**28
-PIECES = 4
+PIECES = 2
 FULL = 60
 AXES = ("section", "expert")
 bf16, f32 = jnp.bfloat16, jnp.float32

time: 108 us -> 107 us (level)
  no operation moved by 1% of the time
where the time goes in v3:
time: 107 us; the launch traced here: 106 us
  starting transfers between devices  47.6 us (44%)
  blocking collectives  24.6 us (23%)
  waiting for transfers between devices  17.8 us (17%)
  Pallas kernels  12.2 us (11%)
  local copies, waits for them, and re-layouts  4.17 us (4%)
    ppermute x8, starting transfers between devices, hop_along(): lax.ppermute(array, 'section', [(i, towards(i, hop, 1)) for i in range(EX...  34.5 us
    all_to_all x1, blocking collectives, per_device(): hidden = exchange(hidden, axis_index_groups=gather_groups)  24.6 us
    all_to_all x1, waiting for transfers between devices, per_device(): parts = exchange(parts, axis_index_groups=wide_groups)  10.5 us
    all_to_all x1, starting transfers between devices, per_device(): parts = exchange(parts, axis_index_groups=wide_groups)  8.3 us
    ppermute x8, waiting for transfers between devices, hop_along(): lax.ppermute(array, 'section', [(i, towards(i, hop, 1)) for i in range(EX...  7.26 us
    pallas_call x2, Pallas kernels, hidden_of(): pl.pallas_call(functools.partial(hidden_kernel, first), out_shape=jax.Sha...  6.9 us
    all_to_all x1, starting transfers between devices, per_device(): down = exchange(down, axis_index_groups=reduce_groups)  4.81 us
    unnamed x24, local copies, waits for them, and re-layouts  4 us
  transfers between devices with their start and end apart: 10, of which 3 were waited for; matrix products, arithmetic and copies ran while one was open for 0% of the time, Pallas kernels for 8%

profile of v3, /device:TPU:1, one launch (start us, length us, event | category | flops | bytes accessed | tf_op | source)
XLA Modules:
  0.0 106.5 jit_solution(2128297622531497406)
XLA Ops:
  0.0 1.1 %copy-done = bf16[1,128,3072]{2,1,0:T(8,128)(2,1)S(1)} copy-done((bf16[1,128,3072]{2,1,0:T(8,128)(2,1)S(1)}, bf16[1,128,3072]{2,1,0:T(8,128)(2,1)}, u32[]{:S(2)}) %copy-start) | copy-done | bytes 786456
  1.1 0.7 copy-done.4
  1.8 0.7 copy-done.6
  2.5 1.1 %shard_map.73 = (bf16[64,3072]{1,0:T(8,128)(2,1)S(1)}, bf16[64,3072]{1,0:T(8,128)(2,1)S(1)}, bf16[64,3072]{1,0:T(8,128)(2,1)S(1)}, bf16[64,3072]{1,0:T(8,128)(2,...) custom-call(bf16[128,3072]{1,0:T(8,128)(2,1)S(1)} %bitcast.12, ...), custom_call_target="tpu_custom_call" | custom-call | tf_op jit(solution)/shard_map/pallas_call | solution.py:242
  3.6 4.0 %collective-permute-start = (bf16[64,3072]{1,0:T(8,128)(2,1)S(1)}, bf16[64,3072]{1,0:T(8,128)(2,1)S(1)}, u32[]{:S(2)}, u32[]{:S(2)}) collective-permute-start(bf16[64,3072]{1,0:T(8,128)(2,1)S(1)} %get-tuple-element.17), channel_id=1, source_target_pairs={{0,128},{64,192},{128,256},{192,320},{256,384},{320,448},{384,0},{... | collective-permute-start | bytes 1179656 | tf_op jit(solution)/shard_map/ppermute | solution.py:42
  7.6 3.2 %collective-permute-start.1 = (bf16[64,3072]{1,0:T(8,128)(2,1)S(1)}, bf16[64,3072]{1,0:T(8,128)(2,1)S(1)}, u32[]{:S(2)}, u32[]{:S(2)}) collective-permute-start(bf16[64,3072]{1,0:T(8,128)(2,1)S(1)} %get-tuple-element.18), channel_id=1, source_target_pairs={{0,384},{64,448},{128,0},{192,64},{256,128},{320,192},{384,256},{4... | collective-permute-start | bytes 1179656 | tf_op jit(solution)/shard_map/ppermute | solution.py:42
  10.8 7.1 %collective-permute-start.2 = (bf16[64,3072]{1,0:T(8,128)(2,1)S(1)}, bf16[64,3072]{1,0:T(8,128)(2,1)S(1)}, u32[]{:S(2)}, u32[]{:S(2)}) collective-permute-start(bf16[64,3072]{1,0:T(8,128)(2,1)S(1)} %get-tuple-element.19), channel_id=1, source_target_pairs={{0,192},{64,128},{128,320},{192,256},{256,448},{320,384},{384,64},... | collective-permute-start | bytes 1179656 | tf_op jit(solution)/shard_map/ppermute | solution.py:42
  17.9 3.5 %collective-permute-start.3 = (bf16[64,3072]{1,0:T(8,128)(2,1)S(1)}, bf16[64,3072]{1,0:T(8,128)(2,1)}, u32[]{:S(2)}, u32[]{:S(2)}) collective-permute-start(bf16[64,3072]{1,0:T(8,128)(2,1)S(1)} %get-tuple-element.23), channel_id=1, source_target_pairs={{0,64},{64,0},{128,192},{192,128},{256,320},{320,256},{384,448},{4... | collective-permute-start | bytes 1179656 | tf_op jit(solution)/shard_map/ppermute | solution.py:42
  21.4 4.9 %collective-permute-start.4 = (bf16[64,3072]{1,0:T(8,128)(2,1)S(1)}, bf16[64,3072]{1,0:T(8,128)(2,1)}, u32[]{:S(2)}, u32[]{:S(2)}) collective-permute-start(bf16[64,3072]{1,0:T(8,128)(2,1)S(1)} %get-tuple-element.24), channel_id=1, source_target_pairs={{0,448},{64,384},{128,64},{192,0},{256,192},{320,128},{384,320},{4... | collective-permute-start | bytes 1179656 | tf_op jit(solution)/shard_map/ppermute | solution.py:42
  26.3 0.0 collective-permute-done.rest_1_
  26.3 1.9 %collective-permute-start.5 = (bf16[64,3072]{1,0:T(8,128)(2,1)S(1)}, bf16[64,3072]{1,0:T(8,128)(2,1)}, u32[]{:S(2)}, u32[]{:S(2)}) collective-permute-start(bf16[64,3072]{1,0:T(8,128)(2,1)S(1)} %get-tuple-element.25), channel_id=1, source_target_pairs={{0,256},{64,320},{128,384},{192,448},{256,0},{320,64},{384,128},{4... | collective-permute-start | bytes 1179656 | tf_op jit(solution)/shard_map/ppermute | solution.py:42
  28.2 0.0 collective-permute-done.1.rest_2_
  28.3 5.0 %collective-permute-start.6 = (bf16[64,3072]{1,0:T(8,128)(2,1)S(1)}, bf16[64,3072]{1,0:T(8,128)(2,1)}, u32[]{:S(2)}, u32[]{:S(2)}) collective-permute-start(bf16[64,3072]{1,0:T(8,128)(2,1)S(1)} %get-tuple-element.26), channel_id=1, source_target_pairs={{0,320},{64,256},{128,448},{192,384},{256,64},{320,0},{384,192},{4... | collective-permute-start | bytes 1179656 | tf_op jit(solution)/shard_map/ppermute | solution.py:42
  33.4 0.7 copy-done.11
  34.1 1.1 %shard_map.74 = bf16[8,48,1024]{2,1,0:T(8,128)(2,1)} custom-call(bf16[48,8192]{1,0:T(8,128)(2,1)S(1)} %bitcast.14), custom_call_target="tpu_custom_call" | custom-call | tf_op jit(solution)/shard_map/pallas_call | solution.py:256
  35.2 4.8 %all-to-all-start = ((bf16[8,48,1024]{2,1,0:T(8,128)(2,1)}), bf16[8,48,1024]{2,1,0:T(8,128)(2,1)S(1)}, u32[]{:S(2)}, u32[]{:S(2)}) async-start(bf16[8,48,1024]{2,1,0:T(8,128)(2,1)} %shard_map.74), calls=%async_computation | async-start | bytes 1572864 | tf_op jit(solution)/shard_map/all_to_all | solution.py:257
  40.0 0.7 shard_map.75
  40.8 0.7 copy-done.8
  41.5 3.8 %shard_map.76.rest_0_ = bf16[8,512,128]{2,1,0:T(8,128)(2,1)} custom-call(bf16[3072,128]{1,0:T(8,128)(2,1)} %bitcast.19, bf16[3072,128]{1,0:T(8,128)(2,1)} %bitcast.21, bf16[64,3072]{1,0:T(8,128)(2,1)} %copy-done.8, bf16[64,3072]{1,0:T(8,128)(2,1)} %copy-done.9, bf16[64,3072]{1,0:T(8,128)(2,1)} %copy-done.10, bf16[64,3072]{1,0:T(8,128)(2,1)} %copy-done.11, ...), custom_call_target="tpu_custom_call" | custom-call | flops 17179869184 | bytes 4194304 | tf_op jit(solution)/shard_map/pallas_call | solution.py:212
  45.3 6.6 %collective-permute-done.4.rest_1_ = bf16[64,3072]{1,0:T(8,128)(2,1)} collective-permute-done((bf16[64,3072]{1,0:T(8,128)(2,1)S(1)}, bf16[64,3072]{1,0:T(8,128)(2,1)}, u32[]{:S(2)}, u32[]{:S(2)}) %collective-permute-start.4) | collective-permute-done | bytes 393248 | tf_op jit(solution)/shard_map/ppermute | solution.py:42
  51.9 3.1 %shard_map.77 = bf16[8,512,128]{2,1,0:T(8,128)(2,1)} custom-call(bf16[3072,128]{1,0:T(8,128)(2,1)} %bitcast.20, bf16[3072,128]{1,0:T(8,128)(2,1)} %bitcast.22, bf16[8,512,128]{2,1,0:T(8,128)(2,1)} %shard_map.76.rest_0_, bf16[64,3072]{1,0:T(8,128)(2,1)} %collective-permute-done.4.rest_1_, ...), custom_call_target="tpu_custom_call", output_to_operand_aliasing={{}: (2, {})} | custom-call | flops 268435456 | bytes 4194304 | tf_op jit(solution)/shard_map/pallas_call | solution.py:212
  55.0 0.0 all-to-all-done.down_ref
  55.0 24.6 %all_to_all.15.hidden_ref = bf16[8,512,128]{2,1,0:T(8,128)(2,1)S(1)} all-to-all(bf16[8,512,128]{2,1,0:T(8,128)(2,1)} %shard_map.77), channel_id=1, replica_groups={{0,8,16,24,32,40,48,56},{128,136,144,152,160,168,176,184},{256,264,272,..., dimensions={0} | all-to-all | bytes 2097152 | tf_op jit(solution)/shard_map/all_to_all | solution.py:264
  79.6 1.4 %shard_map.78 = bf16[32,48,128]{2,1,0:T(8,128)(2,1)} custom-call(bf16[8,48,1024]{2,1,0:T(8,128)(2,1)S(1)} %all-to-all-done.down_ref, bf16[8,512,128]{2,1,0:T(8,128)(2,1)S(1)} %all_to_all.15.hidden_ref), custom_call_target="tpu_custom_call" | custom-call | flops 536870912 | bytes 2097152 | tf_op jit(solution)/shard_map/pallas_call | solution.py:266
  81.0 8.3 %all-to-all-start.2 = ((bf16[32,48,128]{2,1,0:T(8,128)(2,1)}), bf16[32,48,128]{2,1,0:T(8,128)(2,1)S(1)}, u32[]{:S(2)}, u32[]{:S(2)}) async-start(bf16[32,48,128]{2,1,0:T(8,128)(2,1)} %shard_map.78), calls=%async_computation.2 | async-start | bytes 786432 | tf_op jit(solution)/shard_map/all_to_all | solution.py:267
  89.3 10.5 %all-to-all-done.2.parts_ref = bf16[32,48,128]{2,1,0:T(8,128)(2,1)S(1)} async-done(((bf16[32,48,128]{2,1,0:T(8,128)(2,1)}), bf16[32,48,128]{2,1,0:T(8,128)(2,1)S(1)}, u32[]{:S(2)}, u32[]{:S(2)}) %all-to-all-start.2) | async-done | bytes 393248 | tf_op jit(solution)/shard_map/all_to_all | solution.py:267
  99.8 0.1 shard_map.79.mine_ref
  99.9 4.9 %collective-permute-start.7 = (bf16[4,48,128]{2,1,0:T(8,128)(2,1)S(1)}, bf16[4,48,128]{2,1,0:T(8,128)(2,1)S(1)}, u32[]{:S(2)}, u32[]{:S(2)}) collective-permute-start(bf16[4,48,128]{2,1,0:T(8,128)(2,1)S(1)} %shard_map.79.mine_ref), channel_id=1, source_target_pairs={{0,64},{64,0},{128,192},{192,128},{256,320},{320,256},{384,448},{4... | collective-permute-start | bytes 147464 | tf_op jit(solution)/shard_map/ppermute | solution.py:42
  104.8 0.1 constant_dynamic-slice_fusion
  104.9 0.1 copy.9
  105.0 0.7 collective-permute-done.7.theirs_ref
  105.7 0.8 shard_map.80
  (23 shorter events, 0.0 us)
Async XLA Ops:
  0.0 1.1 %copy-start = (bf16[1,128,3072]{2,1,0:T(8,128)(2,1)S(1)}, bf16[1,128,3072]{2,1,0:T(8,128)(2,1)}, u32[]{:S(2)}) copy-start(bf16[1,128,3072]{2,1,0:T(8,128)(2,1)} %param.7) | copy-start | bytes 2359300
  1.1 0.7 copy-start.4
  1.8 0.7 copy-start.6
  2.5 31.6 %copy-start.2 = (bf16[1,48,8192]{2,1,0:T(8,128)(2,1)S(1)}, bf16[1,48,8192]{2,1,0:T(8,128)(2,1)}, u32[]{:S(2)}) copy-start(bf16[1,48,8192]{2,1,0:T(8,128)(2,1)} %param.12) | copy-start | bytes 2359300
  3.6 22.7 %collective-permute-start = (bf16[64,3072]{1,0:T(8,128)(2,1)S(1)}, bf16[64,3072]{1,0:T(8,128)(2,1)S(1)}, u32[]{:S(2)}, u32[]{:S(2)}) collective-permute-start(bf16[64,3072]{1,0:T(8,128)(2,1)S(1)} %get-tuple-element.17), channel_id=1, source_target_pairs={{0,128},{64,192},{128,256},{192,320},{256,384},{320,448},{384,0},{... | collective-permute-start | bytes 1179656 | tf_op jit(solution)/shard_map/ppermute | solution.py:42
  7.6 20.7 %collective-permute-start.1 = (bf16[64,3072]{1,0:T(8,128)(2,1)S(1)}, bf16[64,3072]{1,0:T(8,128)(2,1)S(1)}, u32[]{:S(2)}, u32[]{:S(2)}) collective-permute-start(bf16[64,3072]{1,0:T(8,128)(2,1)S(1)} %get-tuple-element.18), channel_id=1, source_target_pairs={{0,384},{64,448},{128,0},{192,64},{256,128},{320,192},{384,256},{4... | collective-permute-start | bytes 1179656 | tf_op jit(solution)/shard_map/ppermute | solution.py:42
  10.8 22.5 %collective-permute-start.2 = (bf16[64,3072]{1,0:T(8,128)(2,1)S(1)}, bf16[64,3072]{1,0:T(8,128)(2,1)S(1)}, u32[]{:S(2)}, u32[]{:S(2)}) collective-permute-start(bf16[64,3072]{1,0:T(8,128)(2,1)S(1)} %get-tuple-element.19), channel_id=1, source_target_pairs={{0,192},{64,128},{128,320},{192,256},{256,448},{320,384},{384,64},... | collective-permute-start | bytes 1179656 | tf_op jit(solution)/shard_map/ppermute | solution.py:42
  17.9 23.6 %collective-permute-start.3 = (bf16[64,3072]{1,0:T(8,128)(2,1)S(1)}, bf16[64,3072]{1,0:T(8,128)(2,1)}, u32[]{:S(2)}, u32[]{:S(2)}) collective-permute-start(bf16[64,3072]{1,0:T(8,128)(2,1)S(1)} %get-tuple-element.23), channel_id=1, source_target_pairs={{0,64},{64,0},{128,192},{192,128},{256,320},{320,256},{384,448},{4... | collective-permute-start | bytes 1179656 | tf_op jit(solution)/shard_map/ppermute | solution.py:42
  21.4 30.4 %collective-permute-start.4 = (bf16[64,3072]{1,0:T(8,128)(2,1)S(1)}, bf16[64,3072]{1,0:T(8,128)(2,1)}, u32[]{:S(2)}, u32[]{:S(2)}) collective-permute-start(bf16[64,3072]{1,0:T(8,128)(2,1)S(1)} %get-tuple-element.24), channel_id=1, source_target_pairs={{0,448},{64,384},{128,64},{192,0},{256,192},{320,128},{384,320},{4... | collective-permute-start | bytes 1179656 | tf_op jit(solution)/shard_map/ppermute | solution.py:42
  26.3 7.0 %copy-start.9 = (bf16[64,3072]{1,0:T(8,128)(2,1)}, bf16[64,3072]{1,0:T(8,128)(2,1)S(1)}, u32[]{:S(2)}) copy-start(bf16[64,3072]{1,0:T(8,128)(2,1)S(1)} %collective-permute-done.rest_1_) | copy-start | bytes 1179652
  26.3 25.6 %collective-permute-start.5 = (bf16[64,3072]{1,0:T(8,128)(2,1)S(1)}, bf16[64,3072]{1,0:T(8,128)(2,1)}, u32[]{:S(2)}, u32[]{:S(2)}) collective-permute-start(bf16[64,3072]{1,0:T(8,128)(2,1)S(1)} %get-tuple-element.25), channel_id=1, source_target_pairs={{0,256},{64,320},{128,384},{192,448},{256,0},{320,64},{384,128},{4... | collective-permute-start | bytes 1179656 | tf_op jit(solution)/shard_map/ppermute | solution.py:42
  28.3 5.1 %copy-start.10 = (bf16[64,3072]{1,0:T(8,128)(2,1)}, bf16[64,3072]{1,0:T(8,128)(2,1)S(1)}, u32[]{:S(2)}) copy-start(bf16[64,3072]{1,0:T(8,128)(2,1)S(1)} %collective-permute-done.1.rest_2_) | copy-start | bytes 1179652
  28.3 23.6 %collective-permute-start.6 = (bf16[64,3072]{1,0:T(8,128)(2,1)S(1)}, bf16[64,3072]{1,0:T(8,128)(2,1)}, u32[]{:S(2)}, u32[]{:S(2)}) collective-permute-start(bf16[64,3072]{1,0:T(8,128)(2,1)S(1)} %get-tuple-element.26), channel_id=1, source_target_pairs={{0,320},{64,256},{128,448},{192,384},{256,64},{320,0},{384,192},{4... | collective-permute-start | bytes 1179656 | tf_op jit(solution)/shard_map/ppermute | solution.py:42
  33.3 0.7 copy-start.11
  35.2 4.8 %copy-start.1 = (bf16[1,128,3072]{2,1,0:T(8,128)(2,1)S(1)}, bf16[1,128,3072]{2,1,0:T(8,128)(2,1)}, u32[]{:S(2)}) copy-start(bf16[1,128,3072]{2,1,0:T(8,128)(2,1)} %param.7) | copy-start | bytes 2359300
  35.2 4.8 %copy-start.3 = (bf16[3072,8]{0,1:T(8,128)(2,1)S(1)}, bf16[3072,8]{0,1:T(8,128)(2,1)}, u32[]{:S(2)}) copy-start(bf16[3072,8]{0,1:T(8,128)(2,1)} %param.9) | copy-start | bytes 147460
  35.2 4.8 %copy-start.5 = (s32[8,128,2]{1,2,0:T(2,128)S(1)}, s32[8,128,2]{1,2,0:T(2,128)}, u32[]{:S(2)}) copy-start(s32[8,128,2]{1,2,0:T(2,128)} %param.13) | copy-start | bytes 24580
  35.2 4.8 %copy-start.7 = (bf16[3072]{0:T(1024)(128)(2,1)S(1)}, bf16[3072]{0:T(1024)(128)(2,1)}, u32[]{:S(2)}) copy-start(bf16[3072]{0:T(1024)(128)(2,1)} %gain_ref.3) | copy-start | bytes 18436
  35.2 19.8 %all-to-all-start = ((bf16[8,48,1024]{2,1,0:T(8,128)(2,1)}), bf16[8,48,1024]{2,1,0:T(8,128)(2,1)S(1)}, u32[]{:S(2)}, u32[]{:S(2)}) async-start(bf16[8,48,1024]{2,1,0:T(8,128)(2,1)} %shard_map.74), calls=%async_computation | async-start | bytes 1572864 | tf_op jit(solution)/shard_map/all_to_all | solution.py:257
  40.8 0.7 copy-start.8
  81.0 18.8 %all-to-all-start.2 = ((bf16[32,48,128]{2,1,0:T(8,128)(2,1)}), bf16[32,48,128]{2,1,0:T(8,128)(2,1)S(1)}, u32[]{:S(2)}, u32[]{:S(2)}) async-start(bf16[32,48,128]{2,1,0:T(8,128)(2,1)} %shard_map.78), calls=%async_computation.2 | async-start | bytes 786432 | tf_op jit(solution)/shard_map/all_to_all | solution.py:267
  99.9 5.8 %collective-permute-start.7 = (bf16[4,48,128]{2,1,0:T(8,128)(2,1)S(1)}, bf16[4,48,128]{2,1,0:T(8,128)(2,1)S(1)}, u32[]{:S(2)}, u32[]{:S(2)}) collective-permute-start(bf16[4,48,128]{2,1,0:T(8,128)(2,1)S(1)} %shard_map.79.mine_ref), channel_id=1, source_target_pairs={{0,64},{64,0},{128,192},{192,128},{256,320},{320,256},{384,448},{4... | collective-permute-start | bytes 147464 | tf_op jit(solution)/shard_map/ppermute | solution.py:42

commit v4 on v2

--- a/solution.py
+++ b/solution.py
@@ -145,10 +145,10 @@
     for at, group in enumerate(landing):
         for copy in group:
             copy.wait()
-        for k in range(at * piece, (at + 1) * piece, 256):
-            right = jnp.concatenate([gate_ref[k : k + 256], up_ref[k : k + 256]], axis=1)
-            term = jnp.dot(rows_ref[:, k : k + 256], right, preferred_element_type=f32)
-            total = term if total is None else total + term
+        span = pl.ds(at * piece, piece)
+        right = jnp.concatenate([gate_ref[span], up_ref[span]], axis=1)
+        term = jnp.dot(rows_ref[:, span], right, preferred_element_type=f32)
+        total = term if total is None else total + term
     return (jax.nn.silu(total[:, :width]) * total[:, width:]).astype(bf16)
 
 
@@ -171,13 +171,9 @@
 
 def project_kernel(down_ref, hidden_ref, out_ref):
     blocks, cols, depth = down_ref.shape
-    width = hidden_ref.shape[2]
-    total = None
-    for q in range(0, RING, 2):
-        left = down_ref[:, :, q * width : (q + 2) * width].reshape(blocks * cols, 2 * width)
-        right = jnp.concatenate([hidden_ref[q], hidden_ref[q + 1]], axis=1)
-        term = lax.dot_general(left, right, (((1,), (1,)), ((), ())), preferred_element_type=f32)
-        total = term if total is None else total + term
+    left = down_ref[...].reshape(blocks * cols, depth)
+    right = jnp.concatenate([hidden_ref[q] for q in range(RING)], axis=1)
+    total = lax.dot_general(left, right, (((1,), (1,)), ((), ())), preferred_element_type=f32)
     parts = total.astype(bf16).reshape(blocks, cols, -1)
     x = lax.axis_index("section") // 2
     for steps in range(CHIPS):

time: 108 us -> 108 us (level)
  transfers between devices with their start and end apart: 10 -> 10, of which waited for: 3 -> 3; matrix products, arithmetic and copies ran while one was open for 0% -> 0% of each run, Pallas kernels for 8% -> 9%
where the time goes in v4:
time: 108 us; the launch traced here: 107 us
  starting transfers between devices  47.8 us (44%)
  blocking collectives  24.3 us (22%)
  waiting for transfers between devices  17.5 us (16%)
  Pallas kernels  12.7 us (12%)
  local copies, waits for them, and re-layouts  4.17 us (4%)
    ppermute x8, starting transfers between devices, hop_along(): lax.ppermute(array, 'section', [(i, towards(i, hop, 1)) for i in range(EX...  34.5 us
    all_to_all x1, blocking collectives, per_device(): hidden = exchange(hidden, axis_index_groups=gather_groups)  24.3 us
    all_to_all x1, waiting for transfers between devices, per_device(): parts = exchange(parts, axis_index_groups=wide_groups)  10.5 us
    all_to_all x1, starting transfers between devices, per_device(): parts = exchange(parts, axis_index_groups=wide_groups)  8.53 us
    pallas_call x2, Pallas kernels, hidden_of(): pl.pallas_call(functools.partial(hidden_kernel, first), out_shape=jax.Sha...  7.42 us
    ppermute x8, waiting for transfers between devices, hop_along(): lax.ppermute(array, 'section', [(i, towards(i, hop, 1)) for i in range(EX...  6.97 us
    all_to_all x1, starting transfers between devices, per_device(): down = exchange(down, axis_index_groups=reduce_groups)  4.81 us
    unnamed x24, local copies, waits for them, and re-layouts  4 us
  transfers between devices with their start and end apart: 10, of which 3 were waited for; matrix products, arithmetic and copies ran while one was open for 0% of the time, Pallas kernels for 9%

profile of v4, /device:TPU:1, one launch (start us, length us, event | category | flops | bytes accessed | tf_op | source)
XLA Modules:
  0.0 106.7 jit_solution(14202017961003388632)
XLA Ops:
  0.0 1.1 %copy-done = bf16[1,128,3072]{2,1,0:T(8,128)(2,1)S(1)} copy-done((bf16[1,128,3072]{2,1,0:T(8,128)(2,1)S(1)}, bf16[1,128,3072]{2,1,0:T(8,128)(2,1)}, u32[]{:S(2)}) %copy-start) | copy-done | bytes 786456
  1.1 0.7 copy-done.4
  1.8 0.7 copy-done.6
  2.5 1.1 %shard_map.73 = (bf16[64,3072]{1,0:T(8,128)(2,1)S(1)}, bf16[64,3072]{1,0:T(8,128)(2,1)S(1)}, bf16[64,3072]{1,0:T(8,128)(2,1)S(1)}, bf16[64,3072]{1,0:T(8,128)(2,...) custom-call(bf16[128,3072]{1,0:T(8,128)(2,1)S(1)} %bitcast.12, ...), custom_call_target="tpu_custom_call" | custom-call | tf_op jit(solution)/shard_map/pallas_call | solution.py:238
  3.6 4.0 %collective-permute-start = (bf16[64,3072]{1,0:T(8,128)(2,1)S(1)}, bf16[64,3072]{1,0:T(8,128)(2,1)S(1)}, u32[]{:S(2)}, u32[]{:S(2)}) collective-permute-start(bf16[64,3072]{1,0:T(8,128)(2,1)S(1)} %get-tuple-element.17), channel_id=1, source_target_pairs={{0,128},{64,192},{128,256},{192,320},{256,384},{320,448},{384,0},{... | collective-permute-start | bytes 1179656 | tf_op jit(solution)/shard_map/ppermute | solution.py:42
  7.6 3.2 %collective-permute-start.1 = (bf16[64,3072]{1,0:T(8,128)(2,1)S(1)}, bf16[64,3072]{1,0:T(8,128)(2,1)S(1)}, u32[]{:S(2)}, u32[]{:S(2)}) collective-permute-start(bf16[64,3072]{1,0:T(8,128)(2,1)S(1)} %get-tuple-element.18), channel_id=1, source_target_pairs={{0,384},{64,448},{128,0},{192,64},{256,128},{320,192},{384,256},{4... | collective-permute-start | bytes 1179656 | tf_op jit(solution)/shard_map/ppermute | solution.py:42
  10.8 7.1 %collective-permute-start.2 = (bf16[64,3072]{1,0:T(8,128)(2,1)S(1)}, bf16[64,3072]{1,0:T(8,128)(2,1)S(1)}, u32[]{:S(2)}, u32[]{:S(2)}) collective-permute-start(bf16[64,3072]{1,0:T(8,128)(2,1)S(1)} %get-tuple-element.19), channel_id=1, source_target_pairs={{0,192},{64,128},{128,320},{192,256},{256,448},{320,384},{384,64},... | collective-permute-start | bytes 1179656 | tf_op jit(solution)/shard_map/ppermute | solution.py:42
  17.9 3.5 %collective-permute-start.3 = (bf16[64,3072]{1,0:T(8,128)(2,1)S(1)}, bf16[64,3072]{1,0:T(8,128)(2,1)}, u32[]{:S(2)}, u32[]{:S(2)}) collective-permute-start(bf16[64,3072]{1,0:T(8,128)(2,1)S(1)} %get-tuple-element.23), channel_id=1, source_target_pairs={{0,64},{64,0},{128,192},{192,128},{256,320},{320,256},{384,448},{4... | collective-permute-start | bytes 1179656 | tf_op jit(solution)/shard_map/ppermute | solution.py:42
  21.4 4.9 %collective-permute-start.4 = (bf16[64,3072]{1,0:T(8,128)(2,1)S(1)}, bf16[64,3072]{1,0:T(8,128)(2,1)}, u32[]{:S(2)}, u32[]{:S(2)}) collective-permute-start(bf16[64,3072]{1,0:T(8,128)(2,1)S(1)} %get-tuple-element.24), channel_id=1, source_target_pairs={{0,448},{64,384},{128,64},{192,0},{256,192},{320,128},{384,320},{4... | collective-permute-start | bytes 1179656 | tf_op jit(solution)/shard_map/ppermute | solution.py:42
  26.3 0.0 collective-permute-done.rest_1_
  26.3 1.9 %collective-permute-start.5 = (bf16[64,3072]{1,0:T(8,128)(2,1)S(1)}, bf16[64,3072]{1,0:T(8,128)(2,1)}, u32[]{:S(2)}, u32[]{:S(2)}) collective-permute-start(bf16[64,3072]{1,0:T(8,128)(2,1)S(1)} %get-tuple-element.25), channel_id=1, source_target_pairs={{0,256},{64,320},{128,384},{192,448},{256,0},{320,64},{384,128},{4... | collective-permute-start | bytes 1179656 | tf_op jit(solution)/shard_map/ppermute | solution.py:42
  28.2 0.0 collective-permute-done.1.rest_2_
  28.3 5.0 %collective-permute-start.6 = (bf16[64,3072]{1,0:T(8,128)(2,1)S(1)}, bf16[64,3072]{1,0:T(8,128)(2,1)}, u32[]{:S(2)}, u32[]{:S(2)}) collective-permute-start(bf16[64,3072]{1,0:T(8,128)(2,1)S(1)} %get-tuple-element.26), channel_id=1, source_target_pairs={{0,320},{64,256},{128,448},{192,384},{256,64},{320,0},{384,192},{4... | collective-permute-start | bytes 1179656 | tf_op jit(solution)/shard_map/ppermute | solution.py:42
  33.4 0.7 copy-done.11
  34.1 1.1 %shard_map.74 = bf16[8,48,1024]{2,1,0:T(8,128)(2,1)} custom-call(bf16[48,8192]{1,0:T(8,128)(2,1)S(1)} %bitcast.14), custom_call_target="tpu_custom_call" | custom-call | tf_op jit(solution)/shard_map/pallas_call | solution.py:252
  35.2 4.8 %all-to-all-start = ((bf16[8,48,1024]{2,1,0:T(8,128)(2,1)}), bf16[8,48,1024]{2,1,0:T(8,128)(2,1)S(1)}, u32[]{:S(2)}, u32[]{:S(2)}) async-start(bf16[8,48,1024]{2,1,0:T(8,128)(2,1)} %shard_map.74), calls=%async_computation | async-start | bytes 1572864 | tf_op jit(solution)/shard_map/all_to_all | solution.py:253
  40.0 0.7 shard_map.75
  40.8 0.7 copy-done.8
  41.5 0.0 collective-permute-done.3.rest_4_
  41.5 4.1 %shard_map.76.rest_0_ = bf16[8,512,128]{2,1,0:T(8,128)(2,1)} custom-call(bf16[3072,128]{1,0:T(8,128)(2,1)} %bitcast.19, bf16[3072,128]{1,0:T(8,128)(2,1)} %bitcast.21, bf16[64,3072]{1,0:T(8,128)(2,1)} %copy-done.8, bf16[64,3072]{1,0:T(8,128)(2,1)} %copy-done.9, bf16[64,3072]{1,0:T(8,128)(2,1)} %copy-done.10, bf16[64,3072]{1,0:T(8,128)(2,1)} %copy-done.11, ...), custom_call_target="tpu_custom_call" | custom-call | flops 17179869184 | bytes 4194304 | tf_op jit(solution)/shard_map/pallas_call | solution.py:208
  45.6 6.3 %collective-permute-done.4.rest_1_ = bf16[64,3072]{1,0:T(8,128)(2,1)} collective-permute-done((bf16[64,3072]{1,0:T(8,128)(2,1)S(1)}, bf16[64,3072]{1,0:T(8,128)(2,1)}, u32[]{:S(2)}, u32[]{:S(2)}) %collective-permute-start.4) | collective-permute-done | bytes 393248 | tf_op jit(solution)/shard_map/ppermute | solution.py:42
  51.9 3.3 %shard_map.77 = bf16[8,512,128]{2,1,0:T(8,128)(2,1)} custom-call(bf16[3072,128]{1,0:T(8,128)(2,1)} %bitcast.20, bf16[3072,128]{1,0:T(8,128)(2,1)} %bitcast.22, bf16[8,512,128]{2,1,0:T(8,128)(2,1)} %shard_map.76.rest_0_, bf16[64,3072]{1,0:T(8,128)(2,1)} %collective-permute-done.4.rest_1_, ...), custom_call_target="tpu_custom_call", output_to_operand_aliasing={{}: (2, {})} | custom-call | flops 268435456 | bytes 4194304 | tf_op jit(solution)/shard_map/pallas_call | solution.py:208
  55.2 24.3 %all_to_all.15.hidden_ref = bf16[8,512,128]{2,1,0:T(8,128)(2,1)S(1)} all-to-all(bf16[8,512,128]{2,1,0:T(8,128)(2,1)} %shard_map.77), channel_id=1, replica_groups={{0,8,16,24,32,40,48,56},{128,136,144,152,160,168,176,184},{256,264,272,..., dimensions={0} | all-to-all | bytes 2097152 | tf_op jit(solution)/shard_map/all_to_all | solution.py:260
  79.6 1.4 %shard_map.78 = bf16[32,48,128]{2,1,0:T(8,128)(2,1)} custom-call(bf16[8,48,1024]{2,1,0:T(8,128)(2,1)S(1)} %all-to-all-done.down_ref, bf16[8,512,128]{2,1,0:T(8,128)(2,1)S(1)} %all_to_all.15.hidden_ref), custom_call_target="tpu_custom_call" | custom-call | flops 536870912 | bytes 2097152 | tf_op jit(solution)/shard_map/pallas_call | solution.py:262
  81.0 8.5 %all-to-all-start.2 = ((bf16[32,48,128]{2,1,0:T(8,128)(2,1)}), bf16[32,48,128]{2,1,0:T(8,128)(2,1)S(1)}, u32[]{:S(2)}, u32[]{:S(2)}) async-start(bf16[32,48,128]{2,1,0:T(8,128)(2,1)} %shard_map.78), calls=%async_computation.2 | async-start | bytes 786432 | tf_op jit(solution)/shard_map/all_to_all | solution.py:263
  89.6 10.5 %all-to-all-done.2.parts_ref = bf16[32,48,128]{2,1,0:T(8,128)(2,1)S(1)} async-done(((bf16[32,48,128]{2,1,0:T(8,128)(2,1)}), bf16[32,48,128]{2,1,0:T(8,128)(2,1)S(1)}, u32[]{:S(2)}, u32[]{:S(2)}) %all-to-all-start.2) | async-done | bytes 393248 | tf_op jit(solution)/shard_map/all_to_all | solution.py:263
  100.1 0.1 shard_map.79.mine_ref
  100.1 4.9 %collective-permute-start.7 = (bf16[4,48,128]{2,1,0:T(8,128)(2,1)S(1)}, bf16[4,48,128]{2,1,0:T(8,128)(2,1)S(1)}, u32[]{:S(2)}, u32[]{:S(2)}) collective-permute-start(bf16[4,48,128]{2,1,0:T(8,128)(2,1)S(1)} %shard_map.79.mine_ref), channel_id=1, source_target_pairs={{0,64},{64,0},{128,192},{192,128},{256,320},{320,256},{384,448},{4... | collective-permute-start | bytes 147464 | tf_op jit(solution)/shard_map/ppermute | solution.py:42
  105.0 0.1 constant_dynamic-slice_fusion
  105.1 0.1 copy.9
  105.2 0.7 collective-permute-done.7.theirs_ref
  105.9 0.8 shard_map.80
  (23 shorter events, 0.0 us)
Async XLA Ops:
  0.0 1.1 %copy-start = (bf16[1,128,3072]{2,1,0:T(8,128)(2,1)S(1)}, bf16[1,128,3072]{2,1,0:T(8,128)(2,1)}, u32[]{:S(2)}) copy-start(bf16[1,128,3072]{2,1,0:T(8,128)(2,1)} %param.7) | copy-start | bytes 2359300
  1.1 0.7 copy-start.4
  1.8 0.7 copy-start.6
  2.5 31.6 %copy-start.2 = (bf16[1,48,8192]{2,1,0:T(8,128)(2,1)S(1)}, bf16[1,48,8192]{2,1,0:T(8,128)(2,1)}, u32[]{:S(2)}) copy-start(bf16[1,48,8192]{2,1,0:T(8,128)(2,1)} %param.12) | copy-start | bytes 2359300
  3.6 22.7 %collective-permute-start = (bf16[64,3072]{1,0:T(8,128)(2,1)S(1)}, bf16[64,3072]{1,0:T(8,128)(2,1)S(1)}, u32[]{:S(2)}, u32[]{:S(2)}) collective-permute-start(bf16[64,3072]{1,0:T(8,128)(2,1)S(1)} %get-tuple-element.17), channel_id=1, source_target_pairs={{0,128},{64,192},{128,256},{192,320},{256,384},{320,448},{384,0},{... | collective-permute-start | bytes 1179656 | tf_op jit(solution)/shard_map/ppermute | solution.py:42
  7.6 20.7 %collective-permute-start.1 = (bf16[64,3072]{1,0:T(8,128)(2,1)S(1)}, bf16[64,3072]{1,0:T(8,128)(2,1)S(1)}, u32[]{:S(2)}, u32[]{:S(2)}) collective-permute-start(bf16[64,3072]{1,0:T(8,128)(2,1)S(1)} %get-tuple-element.18), channel_id=1, source_target_pairs={{0,384},{64,448},{128,0},{192,64},{256,128},{320,192},{384,256},{4... | collective-permute-start | bytes 1179656 | tf_op jit(solution)/shard_map/ppermute | solution.py:42
  10.8 22.5 %collective-permute-start.2 = (bf16[64,3072]{1,0:T(8,128)(2,1)S(1)}, bf16[64,3072]{1,0:T(8,128)(2,1)S(1)}, u32[]{:S(2)}, u32[]{:S(2)}) collective-permute-start(bf16[64,3072]{1,0:T(8,128)(2,1)S(1)} %get-tuple-element.19), channel_id=1, source_target_pairs={{0,192},{64,128},{128,320},{192,256},{256,448},{320,384},{384,64},... | collective-permute-start | bytes 1179656 | tf_op jit(solution)/shard_map/ppermute | solution.py:42
  17.9 23.6 %collective-permute-start.3 = (bf16[64,3072]{1,0:T(8,128)(2,1)S(1)}, bf16[64,3072]{1,0:T(8,128)(2,1)}, u32[]{:S(2)}, u32[]{:S(2)}) collective-permute-start(bf16[64,3072]{1,0:T(8,128)(2,1)S(1)} %get-tuple-element.23), channel_id=1, source_target_pairs={{0,64},{64,0},{128,192},{192,128},{256,320},{320,256},{384,448},{4... | collective-permute-start | bytes 1179656 | tf_op jit(solution)/shard_map/ppermute | solution.py:42
  21.4 30.4 %collective-permute-start.4 = (bf16[64,3072]{1,0:T(8,128)(2,1)S(1)}, bf16[64,3072]{1,0:T(8,128)(2,1)}, u32[]{:S(2)}, u32[]{:S(2)}) collective-permute-start(bf16[64,3072]{1,0:T(8,128)(2,1)S(1)} %get-tuple-element.24), channel_id=1, source_target_pairs={{0,448},{64,384},{128,64},{192,0},{256,192},{320,128},{384,320},{4... | collective-permute-start | bytes 1179656 | tf_op jit(solution)/shard_map/ppermute | solution.py:42
  26.3 7.0 %copy-start.9 = (bf16[64,3072]{1,0:T(8,128)(2,1)}, bf16[64,3072]{1,0:T(8,128)(2,1)S(1)}, u32[]{:S(2)}) copy-start(bf16[64,3072]{1,0:T(8,128)(2,1)S(1)} %collective-permute-done.rest_1_) | copy-start | bytes 1179652
  26.3 25.6 %collective-permute-start.5 = (bf16[64,3072]{1,0:T(8,128)(2,1)S(1)}, bf16[64,3072]{1,0:T(8,128)(2,1)}, u32[]{:S(2)}, u32[]{:S(2)}) collective-permute-start(bf16[64,3072]{1,0:T(8,128)(2,1)S(1)} %get-tuple-element.25), channel_id=1, source_target_pairs={{0,256},{64,320},{128,384},{192,448},{256,0},{320,64},{384,128},{4... | collective-permute-start | bytes 1179656 | tf_op jit(solution)/shard_map/ppermute | solution.py:42
  28.3 5.1 %copy-start.10 = (bf16[64,3072]{1,0:T(8,128)(2,1)}, bf16[64,3072]{1,0:T(8,128)(2,1)S(1)}, u32[]{:S(2)}) copy-start(bf16[64,3072]{1,0:T(8,128)(2,1)S(1)} %collective-permute-done.1.rest_2_) | copy-start | bytes 1179652
  28.3 23.6 %collective-permute-start.6 = (bf16[64,3072]{1,0:T(8,128)(2,1)S(1)}, bf16[64,3072]{1,0:T(8,128)(2,1)}, u32[]{:S(2)}, u32[]{:S(2)}) collective-permute-start(bf16[64,3072]{1,0:T(8,128)(2,1)S(1)} %get-tuple-element.26), channel_id=1, source_target_pairs={{0,320},{64,256},{128,448},{192,384},{256,64},{320,0},{384,192},{4... | collective-permute-start | bytes 1179656 | tf_op jit(solution)/shard_map/ppermute | solution.py:42
  33.3 0.7 copy-start.11
  35.2 4.8 %copy-start.1 = (bf16[1,128,3072]{2,1,0:T(8,128)(2,1)S(1)}, bf16[1,128,3072]{2,1,0:T(8,128)(2,1)}, u32[]{:S(2)}) copy-start(bf16[1,128,3072]{2,1,0:T(8,128)(2,1)} %param.7) | copy-start | bytes 2359300
  35.2 4.8 %copy-start.3 = (bf16[3072,8]{0,1:T(8,128)(2,1)S(1)}, bf16[3072,8]{0,1:T(8,128)(2,1)}, u32[]{:S(2)}) copy-start(bf16[3072,8]{0,1:T(8,128)(2,1)} %param.9) | copy-start | bytes 147460
  35.2 4.8 %copy-start.5 = (s32[8,128,2]{1,2,0:T(2,128)S(1)}, s32[8,128,2]{1,2,0:T(2,128)}, u32[]{:S(2)}) copy-start(s32[8,128,2]{1,2,0:T(2,128)} %param.13) | copy-start | bytes 24580
  35.2 4.8 %copy-start.7 = (bf16[3072]{0:T(1024)(128)(2,1)S(1)}, bf16[3072]{0:T(1024)(128)(2,1)}, u32[]{:S(2)}) copy-start(bf16[3072]{0:T(1024)(128)(2,1)} %gain_ref.3) | copy-start | bytes 18436
  35.2 20.0 %all-to-all-start = ((bf16[8,48,1024]{2,1,0:T(8,128)(2,1)}), bf16[8,48,1024]{2,1,0:T(8,128)(2,1)S(1)}, u32[]{:S(2)}, u32[]{:S(2)}) async-start(bf16[8,48,1024]{2,1,0:T(8,128)(2,1)} %shard_map.74), calls=%async_computation | async-start | bytes 1572864 | tf_op jit(solution)/shard_map/all_to_all | solution.py:253
  40.8 0.7 copy-start.8
  81.0 19.0 %all-to-all-start.2 = ((bf16[32,48,128]{2,1,0:T(8,128)(2,1)}), bf16[32,48,128]{2,1,0:T(8,128)(2,1)S(1)}, u32[]{:S(2)}, u32[]{:S(2)}) async-start(bf16[32,48,128]{2,1,0:T(8,128)(2,1)} %shard_map.78), calls=%async_computation.2 | async-start | bytes 786432 | tf_op jit(solution)/shard_map/all_to_all | solution.py:263
  100.1 5.8 %collective-permute-start.7 = (bf16[4,48,128]{2,1,0:T(8,128)(2,1)S(1)}, bf16[4,48,128]{2,1,0:T(8,128)(2,1)S(1)}, u32[]{:S(2)}, u32[]{:S(2)}) collective-permute-start(bf16[4,48,128]{2,1,0:T(8,128)(2,1)S(1)} %shard_map.79.mine_ref), channel_id=1, source_target_pairs={{0,64},{64,0},{128,192},{192,128},{256,320},{320,256},{384,448},{4... | collective-permute-start | bytes 147464 | tf_op jit(solution)/shard_map/ppermute | solution.py:42
